TPU v7x, 32 devices: a whole 2x2x4 slice. The times are simulated.
32 devices in a mesh: seq: 16 (over z, y, core), head: 2 (over x).
Axes of the slice: x: 2, y: 2, z: 4, core: 2. Of those that a mesh axis runs over, the one named last changes fastest.
Arguments:
- fast_q: bfloat16 [4096, 4096], P('seq', 'head'), may hold values from -6 to 6
- fast_k: bfloat16 [4096, 4096], P('seq', 'head'), may hold values from -6 to 6
- fast_v: bfloat16 [4096, 4096], P('seq', 'head'), may hold values from -6 to 6
- rates: float32 [8, 4096], P('head', 'seq'), may hold values from 0.02 to 1
- w_gate: bfloat16 [8, 512, 512], P('head'), may hold values from -0.25 to 0.25
- w_up: bfloat16 [8, 512, 512], P('head'), may hold values from -0.25 to 0.25
- w_down: bfloat16 [8, 512, 512], P('head'), may hold values from -0.25 to 0.25
- w_out: bfloat16 [4096, 5120], P('head'), may hold values from -0.09375 to 0.09375
- att_q: bfloat16 [4096, 5120], P('seq', 'head'), may hold values from -5 to 5
- att_k: bfloat16 [4096, 5120], P('seq', 'head'), may hold values from -5 to 5
- att_v: bfloat16 [4096, 5120], P('seq', 'head'), may hold values from -6 to 6
Outputs:
- mixed: bfloat16 [4096, 5120], P('seq', 'head')
- final_weights: bfloat16 [3, 8, 512, 512], P(None, 'head', 'seq')
All inputs are finite; a program needn't handle non-finite values.
Results may differ from a plain program's by a relative error of at most 0.022.
Values may be sent and summed in bfloat16 or wider, within the bound.
A program may use at most 128 MiB of HBM per device.

v0:
```python
import jax
import jax.numpy as jnp
from jax import lax
from jax.sharding import PartitionSpec as P

AD = 128
SPANS = 2
NS_STEPS = 2


NEWTON_COEFFS = (3.4445, -4.775, 2.0315)


def passed_along(block, axis, distance):
    devices = range(lax.axis_size(axis))
    route = [(i - distance, i) for i in devices if i - distance in devices]
    return lax.ppermute(block, axis, route)


def silu_slope(values):
    sigmoid_val = jax.nn.sigmoid(values)
    return sigmoid_val * (1.0 + values * (1.0 - sigmoid_val))


def product(pattern, left_op, right_op):
    return jnp.einsum(pattern, left_op, right_op, preferred_element_type=jnp.float32)


def fast_apply(weights, queries):
    w_first, w_second, w_third = weights
    gate_pre = product("nhi,hij->nhj", queries, w_first)
    up_pre = product("nhi,hij->nhj", queries, w_second)
    activated = (jax.nn.silu(gate_pre) * up_pre).astype(jnp.bfloat16)
    output = product("nhj,hjk->nhk", activated, w_third)
    factor = lax.rsqrt(jnp.mean(output * output, axis=-1, keepdims=True) + 1e-06)
    return (output * factor).astype(jnp.bfloat16)


def gradients(weights, keys_in, values_in, rate_rows):
    w_first, w_second, w_third = weights
    gate_pre = product("nhi,hij->nhj", keys_in, w_first)
    up_pre = product("nhi,hij->nhj", keys_in, w_second)
    activated = (jax.nn.silu(gate_pre) * up_pre).astype(jnp.bfloat16)
    weighted = (rate_rows[:, :, None] * values_in.astype(jnp.float32)).astype(jnp.bfloat16)
    grad_third = -product("nhj,nhk->hjk", activated, weighted)
    back = -product("nhk,hjk->nhj", weighted, w_third)
    up_in = (back * jax.nn.silu(gate_pre)).astype(jnp.bfloat16)
    gate_in = (back * up_pre * silu_slope(gate_pre)).astype(jnp.bfloat16)
    grad_first = product("nhi,nhj->hij", keys_in, gate_in)
    grad_second = product("nhi,nhj->hij", keys_in, up_in)
    return (grad_first, grad_second, grad_third)


def scale_down(summed):
    squares = jnp.sum(summed * summed, axis=(1, 2))
    return (summed / jnp.sqrt(squares + 1e-06)[:, None, None]).astype(jnp.bfloat16)


def newton_schulz(matrix):
    first, second, third = NEWTON_COEFFS
    for iteration in range(NS_STEPS):
        gram = product("mij,mkj->mik", matrix, matrix).astype(jnp.bfloat16)
        square = product("mij,mjk->mik", gram, gram)
        poly = (second * gram.astype(jnp.float32) + third * square).astype(jnp.bfloat16)
        matrix = (
            first * matrix.astype(jnp.float32) + product("mij,mjk->mik", poly, matrix)
        ).astype(jnp.bfloat16)
    return matrix


def renorm(weight, ortho):
    unmoved = weight.astype(jnp.float32)
    moved = unmoved - ortho.astype(jnp.float32)
    target = jnp.sqrt(jnp.sum(unmoved * unmoved, axis=1, keepdims=True) + 1e-06)
    current = jnp.sqrt(jnp.sum(moved * moved, axis=1, keepdims=True) + 1e-06)
    return (moved * (target / current)).astype(jnp.bfloat16)


def attend(queries, keys_all, values_all, offset, window):
    block = queries.shape[0]
    scores = product("qhd,khd->hqk", queries, keys_all) * queries.shape[-1] ** (-0.5)
    query_pos = offset + lax.broadcasted_iota(jnp.int32, (block, 2 * block), 0)
    key_pos = offset - block + lax.broadcasted_iota(jnp.int32, (block, 2 * block), 1)
    allowed = (key_pos <= query_pos) & (key_pos > query_pos - window) & (key_pos >= 0)
    scores = jnp.where(allowed[None], scores, -1e30)
    row_max = jnp.max(scores, axis=-1, keepdims=True)
    exp_scores = jnp.exp(scores - row_max)
    probs = (exp_scores / jnp.sum(exp_scores, axis=-1, keepdims=True)).astype(jnp.bfloat16)
    return product("hqk,khd->qhd", probs, values_all)


def on_device(fast_q, fast_k, fast_v, rates, w_gate, w_up, w_down, w_out, att_q, att_k, att_v):
    row_count = fast_q.shape[0]
    heads_here = w_gate.shape[0]
    feature_count = w_gate.shape[1]
    queries = fast_q.reshape(row_count, heads_here, feature_count)
    keys_fast = fast_k.reshape(row_count, heads_here, feature_count)
    values_fast = fast_v.reshape(row_count, heads_here, feature_count)
    rate_rows = rates.T
    seq_count = lax.axis_size("seq")
    position = lax.axis_index("seq")
    group_id = position // (seq_count // SPANS)
    weights = (w_gate, w_up, w_down)
    chosen = weights
    for span in range(SPANS):
        grads = gradients(weights, keys_fast, values_fast, rate_rows)
        stacked = jnp.concatenate(grads, axis=0)
        stacked = jnp.where(group_id == span, stacked, jnp.zeros_like(stacked))
        summed = lax.psum(stacked.astype(jnp.bfloat16), "seq").astype(jnp.float32)
        start_matrix = scale_down(summed)
        ortho = newton_schulz(start_matrix)
        pieces = ortho.reshape(3, heads_here, feature_count, feature_count)
        weights = tuple((renorm(weights[member], pieces[member]) for member in range(3)))
        if span + 1 < SPANS:
            chosen = tuple(
                (
                    jnp.where(group_id == span + 1, fresh, older)
                    for fresh, older in zip(weights, chosen)
                )
            )
    row_share = feature_count // seq_count
    final_all = jnp.stack(weights, axis=0)
    final_weights = lax.dynamic_slice_in_dim(final_all, position * row_share, row_share, 2)
    fast_rows = fast_apply(chosen, queries).reshape(row_count, heads_here * feature_count)
    partial_out = jnp.dot(fast_rows, w_out, preferred_element_type=jnp.float32)
    fast_sum = lax.psum_scatter(
        partial_out.astype(jnp.bfloat16), "head", scatter_dimension=1, tiled=True
    ).astype(jnp.float32)
    att_heads = att_q.shape[1] // AD
    queries_att = att_q.reshape(row_count, att_heads, AD)
    keys_att = att_k.reshape(row_count, att_heads, AD)
    values_att = att_v.reshape(row_count, att_heads, AD)
    prior = passed_along((keys_att, values_att), "seq", 1)
    keys_all = jnp.concatenate([prior[0], keys_att], axis=0)
    values_all = jnp.concatenate([prior[1], values_att], axis=0)
    attended = attend(queries_att, keys_all, values_all, position * row_count, row_count)
    attended = attended.reshape(row_count, att_heads * AD)
    return ((attended + fast_sum).astype(jnp.bfloat16), final_weights)


def solution(mesh):
    in_specs = (
        P("seq", "head"),
        P("seq", "head"),
        P("seq", "head"),
        P("head", "seq"),
        P("head", None, None),
        P("head", None, None),
        P("head", None, None),
        P("head", None),
        P("seq", "head"),
        P("seq", "head"),
        P("seq", "head"),
    )
    out_specs = (P("seq", "head"), P(None, "head", "seq", None))
    return jax.shard_map(
        on_device, mesh=mesh, in_specs=in_specs, out_specs=out_specs, check_vma=False
    )
```

profile of v0, /device:TPU:11, one launch (start us, length us, event | category | flops | bytes accessed | tf_op | source)
XLA Modules:
  0.0 495.6 jit_solution(2723281269652981797)
XLA Ops:
  10.3 3.7 collective-permute-start.1
  32.2 6.8 %fusion.5 = bf16[12,512,512]{1,2,0:T(8,128)(2,1)} fusion(bf16[4,512,512]{1,2,0:T(8,128)(2,1)} %convolution_negate_fusion.1, bf16[4,512,512]{1,2,0:T(8,128)(2,1)} %convolution_bitcast_fusion.2, bf16[4,512,512]{1,2,0:T(8,128)(2,1)} %convolution_bitcast_fusion.3, pred[]{:T(512)S(6)} %eq.10), kind=kLoop, calls=%fused_computation.10 | loop fusion | flops 22020096 | bytes 12582913 | tf_op jit(solution)/shard_map/convert_element_type | solution.py:109
  44.5 4.6 copy.74
  53.3 7.1 %fusion.33 = f32[20,512,256]{2,1,0:T(8,128)} fusion(bf16[256,20,128]{0,2,1:T(8,128)(2,1)S(1)} %bitcast.216, bf16[256,20,128]{2,0,1:T(8,128)(2,1)} %copy.69, bf16[256,20,128]{2,0,1:T(8,128)(2,1)} %collective-permute-done.1), kind=kOutput, calls=%fused_computation.82 | convolution fusion | flops 676331520 | bytes 14417920 | tf_op jit(solution)/shard_map/qhd,khd->hqk/dot_general | solution.py:26
  60.4 15.4 %fusion.140 = (f32[20,256]{1,0:T(8,128)S(1)}, f32[20,256,512]{1,2,0:T(8,128)}) fusion(f32[20,512,256]{2,1,0:T(8,128)} %fusion.33, pred[256,512]{0,1:T(8,128)(4,1)S(1)} %and_and_fusion), kind=kOutput, calls=%fused_computation.209 | output fusion | flops 15729151 | bytes 21123072 | tf_op jit(solution)/shard_map/sub | solution.py:87
  75.9 7.1 %fusion.22 = f32[20,128,256]{2,1,0:T(8,128)} fusion(f32[20,256,512]{1,2,0:T(8,128)} %get-tuple-element.25, f32[20,256]{1,0:T(8,128)S(1)} %get-tuple-element.24, bf16[256,20,128]{0,2,1:T(8,128)(2,1)S(1)} %bitcast.222, bf16[256,20,128]{0,2,1:T(8,128)(2,1)} %collective-permute-done), kind=kOutput, calls=%fused_computation.55 | convolution fusion | flops 681574400 | bytes 15749120 | tf_op jit(solution)/shard_map/hqk,khd->qhd/dot_general | solution.py:26
  86.5 91.7 %all-reduce.3.cloned.1.call-done = bf16[12,512,512]{1,2,0:T(8,128)(2,1)} async-done(((bf16[12,512,512]{1,2,0:T(8,128)(2,1)}), bf16[12,512,512]{1,2,0:T(8,128)(2,1)}) %all-reduce.3.cloned.1.call-update) | async-done | bytes 6291472 | tf_op jit(solution)/shard_map/psum | solution.py:109
  178.2 4.2 fusion.1
  182.4 11.1 %convolution_convert_fusion.4 = bf16[12,512,512]{2,1,0:T(8,128)(2,1)} fusion(bf16[12,512,512]{1,2,0:T(8,128)(2,1)} %all-reduce.3.cloned.1.call-done, f32[12]{0:T(128)S(1)} %add_sqrt_fusion.1), kind=kOutput, calls=%fused_computation.78 | convolution fusion | flops 3233808384 | bytes 12582960 | tf_op jit(solution)/shard_map/mij,mkj->mik/dot_general | solution.py:26
  193.5 19.4 %add_convert_fusion.6 = bf16[12,512,512]{1,2,0:T(8,128)(2,1)} fusion(bf16[12,512,512]{2,1,0:T(8,128)(2,1)} %convolution_convert_fusion.4, f32[12]{0:T(128)S(1)} %add_sqrt_fusion.1, bf16[12,512,512]{1,2,0:T(8,128)(2,1)} %all-reduce.3.cloned.1.call-done), kind=kOutput, calls=%fused_computation.19 | convolution fusion | flops 6489636864 | bytes 18874416 | tf_op jit(solution)/shard_map/mij,mjk->mik/dot_general | solution.py:26
  213.0 10.7 %convolution_convert_fusion.3 = bf16[12,512,512]{2,1,0:T(8,128)(2,1)} fusion(bf16[12,512,512]{1,2,0:T(8,128)(2,1)} %add_convert_fusion.6), kind=kOutput, calls=%fused_computation.77 | convolution fusion | flops 3224371200 | bytes 12582912 | tf_op jit(solution)/shard_map/mij,mkj->mik/dot_general | solution.py:26
  223.7 19.3 %add_convert_fusion.4 = bf16[12,512,512]{1,2,0:T(8,128)(2,1)} fusion(bf16[12,512,512]{1,2,0:T(8,128)(2,1)} %add_convert_fusion.6, bf16[12,512,512]{2,1,0:T(8,128)(2,1)} %convolution_convert_fusion.3), kind=kOutput, calls=%fused_computation.17 | convolution fusion | flops 6470762496 | bytes 18874368 | tf_op jit(solution)/shard_map/mij,mjk->mik/dot_general | solution.py:26
  243.0 5.7 %multiply_reduce_fusion.4 = (f32[4,512]{1,0:T(4,128)S(1)}, f32[4,512]{1,0:T(4,128)S(1)}, f32[4,512]{1,0:T(4,128)S(1)}, f32[4,512]{1,0:T(4,128)S(1)}, f32[4,512]{1,0:T(4,128)S(1)}, /*index=5*/f32[4,512]{1,0:T(4,128)S(1)}) fusion(bf16[4,512,512]{1,2,0:T(8,128)(2,1)} %copy.97, bf16[12,512,512]{1,2,0:T(8,128)(2,1)} %add_convert_fusion.4, ...), kind=kLoop, calls=%fused_computation.72 | loop fusion | flops 22007808 | bytes 12632064 | tf_op jit(solution)/shard_map/reduce_sum | solution.py:75
  250.1 3.7 multiply_convert_fusion.4
  262.8 5.5 %fusion.6 = bf16[12,512,512]{1,2,0:T(8,128)(2,1)} fusion(bf16[4,512,512]{1,2,0:T(8,128)(2,1)S(1)} %convolution_negate_fusion, bf16[4,512,512]{1,2,0:T(8,128)(2,1)S(1)} %convolution_bitcast_fusion, bf16[4,512,512]{1,2,0:T(8,128)(2,1)S(1)} %convolution_bitcast_fusion.1, pred[]{:T(512)S(6)} %eq.4), kind=kLoop, calls=%fused_computation.12 | loop fusion | flops 22020096 | bytes 12582913 | tf_op jit(solution)/shard_map/convert_element_type | solution.py:109
  268.4 5.7 %fusion.58 = (f32[256,4]{0,1:T(4,128)S(1)}, f32[4,512,256]{2,1,0:T(8,128)}) fusion(f32[4,512,256]{1,2,0:T(8,128)} %fusion.73, bf16[256,4,512]{0,2,1:T(8,128)(2,1)S(1)} %bitcast.219, bf16[4,512,512]{1,2,0:T(8,128)(2,1)} %copy-done, bf16[4,512,512]{1,2,0:T(8,128)(2,1)} %copy.97, pred[]{:T(512)S(6)} %eq.4, bf16[4,512,512]{1,2,0:T(8,128)(2,1)} %copy-done.2, ...), kind=kOutput, calls=%fused_computation.119 | convolution fusion | flops 1080032256 | bytes 13635585 | tf_op jit(solution)/shard_map/nhj,hjk->nhk/dot_general | solution.py:26
  276.3 14.3 %convolution_convert_fusion = bf16[256,5120]{1,0:T(8,128)(2,1)} fusion(bf16[256,2048]{0,1:T(8,128)(2,1)S(1)} %bitcast.215, bf16[2048,5120]{1,0:T(8,128)(2,1)} %param.18), kind=kOutput, calls=%fused_computation.25 | convolution fusion | flops 5370019840 | bytes 24641536 | tf_op jit(solution)/shard_map/dot_general | solution.py:125
  290.7 116.9 %all-reduce.5.cloned.1.call-done = bf16[12,512,512]{1,2,0:T(8,128)(2,1)} async-done(((bf16[12,512,512]{1,2,0:T(8,128)(2,1)}), bf16[12,512,512]{1,2,0:T(8,128)(2,1)}) %all-reduce.5.cloned.1.call-update) | async-done | bytes 6291472 | tf_op jit(solution)/shard_map/psum | solution.py:109
  407.5 4.2 fusion.3
  411.7 11.1 %convolution_convert_fusion.2 = bf16[12,512,512]{2,1,0:T(8,128)(2,1)} fusion(bf16[12,512,512]{1,2,0:T(8,128)(2,1)} %all-reduce.5.cloned.1.call-done, f32[12]{0:T(128)S(1)} %add_sqrt_fusion), kind=kOutput, calls=%fused_computation.76 | convolution fusion | flops 3233808384 | bytes 12582960 | tf_op jit(solution)/shard_map/mij,mkj->mik/dot_general | solution.py:26
  422.8 19.9 %add_convert_fusion.2 = bf16[12,512,512]{1,2,0:T(8,128)(2,1)} fusion(bf16[12,512,512]{2,1,0:T(8,128)(2,1)} %convolution_convert_fusion.2, f32[12]{0:T(128)S(1)} %add_sqrt_fusion, bf16[12,512,512]{1,2,0:T(8,128)(2,1)} %all-reduce.5.cloned.1.call-done), kind=kOutput, calls=%fused_computation.15 | convolution fusion | flops 6489636864 | bytes 18874416 | tf_op jit(solution)/shard_map/mij,mjk->mik/dot_general | solution.py:26
  442.8 10.8 %convolution_convert_fusion.1 = bf16[12,512,512]{2,1,0:T(8,128)(2,1)} fusion(bf16[12,512,512]{1,2,0:T(8,128)(2,1)} %add_convert_fusion.2), kind=kOutput, calls=%fused_computation.75 | convolution fusion | flops 3224371200 | bytes 12582912 | tf_op jit(solution)/shard_map/mij,mkj->mik/dot_general | solution.py:26
  453.6 19.3 %add_convert_fusion = bf16[12,512,512]{1,2,0:T(8,128)(2,1)} fusion(bf16[12,512,512]{1,2,0:T(8,128)(2,1)} %add_convert_fusion.2, bf16[12,512,512]{2,1,0:T(8,128)(2,1)} %convolution_convert_fusion.1), kind=kOutput, calls=%fused_computation.13 | convolution fusion | flops 6470762496 | bytes 18874368 | tf_op jit(solution)/shard_map/mij,mjk->mik/dot_general | solution.py:26
  472.9 6.7 %multiply_reduce_fusion = (f32[4,512]{1,0:T(4,128)S(1)}, f32[4,512]{1,0:T(4,128)S(1)}, f32[4,512]{1,0:T(4,128)S(1)}, f32[4,512]{1,0:T(4,128)S(1)}, f32[4,512]{1,0:T(4,128)S(1)}, /*index=5*/f32[4,512]{1,0:T(4,128)S(1)}) fusion(bf16[4,512,512]{1,2,0:T(8,128)(2,1)} %copy-done.2, bf16[12,512,512]{1,2,0:T(8,128)(2,1)} %add_convert_fusion, ...), kind=kLoop, calls=%fused_computation.64 | loop fusion | flops 22007808 | bytes 12632064 | tf_op jit(solution)/shard_map/reduce_sum | solution.py:75
  (90 shorter events, 55.9 us)
Async XLA Ops:
  7.2 171.0 %all-reduce.3.cloned.1.call-start = ((), (), s32[]{:S(2)}) async-start(), calls=%async_computation.1 | async-start | bytes 12582912 | tf_op jit(solution)/shard_map/psum | solution.py:109
  8.8 11.1 %copy-start.10 = (bf16[256,2048]{1,0:T(8,128)(2,1)S(1)}, bf16[256,2048]{1,0:T(8,128)(2,1)}, u32[]{:S(2)}) copy-start(bf16[256,2048]{1,0:T(8,128)(2,1)} %param.12) | copy-start | bytes 3145732
  10.3 43.0 %collective-permute-start.1 = (bf16[256,20,128]{2,0,1:T(8,128)(2,1)}, bf16[256,20,128]{2,0,1:T(8,128)(2,1)}, u32[]{:S(2)}, u32[]{:S(2)}) collective-permute-start(bf16[256,20,128]{2,0,1:T(8,128)(2,1)} %copy.69), channel_id=1, source_target_pairs={{0,2},{2,4},{4,6},{6,8},{8,10},{10,12},{12,14},{14,16},{16,18},{18... | collective-permute-start | bytes 3932168 | tf_op jit(solution)/shard_map/ppermute | solution.py:17
  16.4 5.8 %copy-start.15 = (bf16[4,512,512]{2,1,0:T(8,128)(2,1)S(1)}, bf16[4,512,512]{2,1,0:T(8,128)(2,1)}, u32[]{:S(2)}) copy-start(bf16[4,512,512]{2,1,0:T(8,128)(2,1)} %param.15) | copy-start | bytes 6291460
  16.4 59.4 %collective-permute-start = (bf16[256,20,128]{0,2,1:T(8,128)(2,1)}, bf16[256,20,128]{0,2,1:T(8,128)(2,1)}, u32[]{:S(2)}, u32[]{:S(2)}) collective-permute-start(bf16[256,20,128]{0,2,1:T(8,128)(2,1)} %bitcast.221), channel_id=1, source_target_pairs={{0,2},{2,4},{4,6},{6,8},{8,10},{10,12},{12,14},{14,16},{16,18},{18... | collective-permute-start | bytes 3932168 | tf_op jit(solution)/shard_map/ppermute | solution.py:17
  19.9 3.1 copy-start.19
  22.3 1.6 copy-start.16
  39.1 368.4 %all-reduce.5.cloned.1.call-start = ((), (), s32[]{:S(2)}) async-start(), calls=%async_computation.3 | async-start | bytes 12582912 | tf_op jit(solution)/shard_map/psum | solution.py:109
  44.5 198.5 %copy-start.4 = (bf16[4,512,512]{1,2,0:T(8,128)(2,1)}, bf16[4,512,512]{1,2,0:T(8,128)(2,1)S(1)}, u32[]{:S(2)}) copy-start(bf16[4,512,512]{1,2,0:T(8,128)(2,1)S(1)} %copy.101) | copy-start | bytes 6291460
  60.4 15.5 %copy-start.18 = (bf16[256,2560]{0,1:T(8,128)(2,1)S(1)}, bf16[256,2560]{0,1:T(8,128)(2,1)}, u32[]{:S(2)}) copy-start(bf16[256,2560]{0,1:T(8,128)(2,1)} %copy.67) | copy-start | bytes 3932164
  243.0 5.9 %copy-start.7 = (bf16[12,512,512]{1,2,0:T(8,128)(2,1)S(1)}, bf16[12,512,512]{1,2,0:T(8,128)(2,1)}, u32[]{:S(2)}) copy-start(bf16[12,512,512]{1,2,0:T(8,128)(2,1)} %add_convert_fusion.4) | copy-start | bytes 18874372
  243.0 6.5 %copy-start.8 = (bf16[4,512,512]{1,2,0:T(8,128)(2,1)S(1)}, bf16[4,512,512]{1,2,0:T(8,128)(2,1)}, u32[]{:S(2)}) copy-start(bf16[4,512,512]{1,2,0:T(8,128)(2,1)} %copy.97) | copy-start | bytes 6291460
  243.0 7.1 %copy-start.9 = (bf16[4,512,512]{1,2,0:T(8,128)(2,1)S(1)}, bf16[4,512,512]{1,2,0:T(8,128)(2,1)}, u32[]{:S(2)}) copy-start(bf16[4,512,512]{1,2,0:T(8,128)(2,1)} %copy.74) | copy-start | bytes 6291460
  250.1 3.7 copy-start.11
  253.8 1.5 copy-start
  253.8 2.0 copy-start.2
  253.8 2.0 copy-start.14
  258.7 1.6 copy-start.5
  258.7 1.9 copy-start.17
  268.3 217.6 %reduce-scatter.2.cloned.1.call-start = ((), (), s32[]{:S(2)}) async-start(), calls=%async_computation.2 | async-start | bytes 3932160 | tf_op jit(solution)/shard_map/reduce_scatter | solution.py:126
  472.9 6.8 %copy-start.1 = (bf16[4,512,512]{1,2,0:T(8,128)(2,1)S(1)}, bf16[4,512,512]{1,2,0:T(8,128)(2,1)}, u32[]{:S(2)}) copy-start(bf16[4,512,512]{1,2,0:T(8,128)(2,1)} %copy-done) | copy-start | bytes 6291460
  472.9 6.8 %copy-start.3 = (bf16[4,512,512]{1,2,0:T(8,128)(2,1)S(1)}, bf16[4,512,512]{1,2,0:T(8,128)(2,1)}, u32[]{:S(2)}) copy-start(bf16[4,512,512]{1,2,0:T(8,128)(2,1)} %copy-done.2) | copy-start | bytes 6291460
  472.9 7.1 %copy-start.6 = (bf16[12,512,512]{1,2,0:T(8,128)(2,1)S(1)}, bf16[12,512,512]{1,2,0:T(8,128)(2,1)}, u32[]{:S(2)}) copy-start(bf16[12,512,512]{1,2,0:T(8,128)(2,1)} %add_convert_fusion) | copy-start | bytes 18874372
  481.9 4.0 copy-start.12
  (1 other events, 1.0 us)
Sparse Core Ops, SparseCore 0:
  39.2 138.9 all-reduce.2
  268.4 139.0 all-reduce.4
  409.8 36.7 reduce-scatter.1
where the time goes:
time: 504 us; the launch traced here: 496 us
  waiting for transfers between devices  209 us (41%)
  matrix products  175 us (35%)
  other arithmetic  62.8 us (12%)
  local copies, waits for them, and re-layouts  28.6 us (6%)
  between operations  14.6 us (3%)
  starting transfers between devices  6.07 us (1%)
    psum x2, waiting for transfers between devices, on_device(): summed = lax.psum(stacked.astype(jnp.bfloat16), 'seq').astype(jnp.float32)  209 us
    dot_general x24, matrix products, product(): jnp.einsum(pattern, left_op, right_op, preferred_element_type=jnp.float32)  161 us
    unnamed x47, local copies, waits for them, and re-layouts  21.3 us
    sub x1, other arithmetic, attend(): exp_scores = jnp.exp(scores - row_max)  15.4 us
    dot_general x1, matrix products, on_device(): partial_out = jnp.dot(fast_rows, w_out, preferred_element_type=jnp.float32)  14.3 us
    reduce_sum x2, other arithmetic, renorm(): current = jnp.sqrt(jnp.sum(moved * moved, axis=1, keepdims=True) + 1e-06)  12.5 us
    convert_element_type x2, other arithmetic, on_device(): summed = lax.psum(stacked.astype(jnp.bfloat16), 'seq').astype(jnp.float32)  12.3 us
  transfers between devices with their start and end apart: 5, of which 2 were waited for; matrix products, arithmetic and copies ran while one was open for 34% of the time, Pallas kernels for 0%

commit v1 on v0

--- a/solution.py
+++ b/solution.py
@@ -1,11 +1,18 @@
+import functools
+
 import jax
 import jax.numpy as jnp
 from jax import lax
+from jax.experimental import pallas as pl
+from jax.experimental.pallas import tpu as pltpu
 from jax.sharding import PartitionSpec as P
 
 AD = 128
 SPANS = 2
 NS_STEPS = 2
+MESH = pl.DeviceIdType.MESH
+VMEM_LIMIT = 52 * 1024 * 1024
+KINDS = 3
 
 
 NEWTON_COEFFS = (3.4445, -4.775, 2.0315)
@@ -138,6 +145,430 @@
     return ((attended + fast_sum).astype(jnp.bfloat16), final_weights)
 
 
+def dot_on(left, right, left_dim, right_dim):
+    return lax.dot_general(
+        left, right, (((left_dim,), (right_dim,)), ((), ())), preferred_element_type=jnp.float32
+    )
+
+
+def gradient_body(k_ref, v_ref, r_ref, wg_ref, wu_ref, wd_ref, g_ref):
+    keys_in = k_ref[...]
+    gate_pre = dot_on(keys_in, wg_ref[0], 1, 0)
+    up_pre = dot_on(keys_in, wu_ref[0], 1, 0)
+    weighted = (r_ref[0] * v_ref[...].astype(jnp.float32)).astype(jnp.bfloat16)
+    back = -dot_on(weighted, wd_ref[0], 1, 1)
+    sigmoid_val = 1.0 / (1.0 + jnp.exp(-gate_pre))
+    silu_val = gate_pre * sigmoid_val
+    activated = (silu_val * up_pre).astype(jnp.bfloat16)
+    up_in = (back * silu_val).astype(jnp.bfloat16)
+    slope = sigmoid_val * (1.0 + gate_pre * (1.0 - sigmoid_val))
+    gate_in = (back * up_pre * slope).astype(jnp.bfloat16)
+    g_ref[0, 0] = dot_on(keys_in, gate_in, 0, 0).astype(jnp.bfloat16)
+    g_ref[1, 0] = dot_on(keys_in, up_in, 0, 0).astype(jnp.bfloat16)
+    g_ref[2, 0] = -dot_on(activated, weighted, 0, 0).astype(jnp.bfloat16)
+
+
+def gradient_call(weights, keys_in, values_in, rate_cols):
+    heads, feature, _ = weights[0].shape
+    rows = keys_in.shape[0]
+    rows_spec = pl.BlockSpec((rows, feature), lambda h: (0, h))
+    weight_spec = pl.BlockSpec((1, feature, feature), lambda h: (h, 0, 0))
+    return pl.pallas_call(
+        gradient_body,
+        grid=(heads,),
+        in_specs=[rows_spec, rows_spec, pl.BlockSpec((1, rows, 1), lambda h: (h, 0, 0))]
+        + [weight_spec] * KINDS,
+        out_specs=pl.BlockSpec((KINDS, 1, feature, feature), lambda h: (0, h, 0, 0)),
+        out_shape=jax.ShapeDtypeStruct((KINDS, heads, feature, feature), jnp.bfloat16),
+        compiler_params=pltpu.CompilerParams(vmem_limit_bytes=VMEM_LIMIT),
+        name="gradients",
+    )(keys_in, values_in, rate_cols, *weights)
+
+
+def apply_body(q_ref, wg_ref, wu_ref, wd_ref, o_ref):
+    queries = q_ref[...]
+    gate_pre = dot_on(queries, wg_ref[0], 1, 0)
+    up_pre = dot_on(queries, wu_ref[0], 1, 0)
+    activated = (gate_pre / (1.0 + jnp.exp(-gate_pre)) * up_pre).astype(jnp.bfloat16)
+    output = dot_on(activated, wd_ref[0], 1, 0)
+    factor = lax.rsqrt(jnp.mean(output * output, axis=-1, keepdims=True) + 1e-06)
+    o_ref[...] = (output * factor).astype(jnp.bfloat16)
+
+
+def apply_call(weights, queries):
+    heads, feature, _ = weights[0].shape
+    rows = queries.shape[0]
+    rows_spec = pl.BlockSpec((rows, feature), lambda h: (0, h))
+    weight_spec = pl.BlockSpec((1, feature, feature), lambda h: (h, 0, 0))
+    return pl.pallas_call(
+        apply_body,
+        grid=(heads,),
+        in_specs=[rows_spec] + [weight_spec] * KINDS,
+        out_specs=rows_spec,
+        out_shape=jax.ShapeDtypeStruct(queries.shape, jnp.bfloat16),
+        compiler_params=pltpu.CompilerParams(vmem_limit_bytes=VMEM_LIMIT),
+        name="fast_apply",
+    )(queries, *weights)
+
+
+def attention_body(q_ref, kp_ref, vp_ref, k_ref, v_ref, o_ref):
+    rows = q_ref.shape[0]
+    first = lax.axis_index("seq") == 0
+    row = lax.broadcasted_iota(jnp.int32, (rows, rows), 0)
+    col = lax.broadcasted_iota(jnp.int32, (rows, rows), 1)
+    column_floor = jnp.where(first, rows, 0)
+    prior_ok = (col > row) & (col >= column_floor)
+    own_ok = col <= row
+    for head in range(q_ref.shape[1] // AD):
+        lanes = slice(head * AD, (head + 1) * AD)
+        queries = q_ref[:, lanes]
+        prior = dot_on(queries, kp_ref[:, lanes], 1, 1) * AD ** (-0.5)
+        own = dot_on(queries, k_ref[:, lanes], 1, 1) * AD ** (-0.5)
+        prior = jnp.where(prior_ok, prior, -1e30)
+        own = jnp.where(own_ok, own, -1e30)
+        top = jnp.max(jnp.maximum(prior, own), axis=-1, keepdims=True)
+        prior = jnp.exp(prior - top)
+        own = jnp.exp(own - top)
+        scale = 1.0 / jnp.sum(prior + own, axis=-1, keepdims=True)
+        prior = (prior * scale).astype(jnp.bfloat16)
+        own = (own * scale).astype(jnp.bfloat16)
+        o_ref[:, lanes] = (
+            dot_on(prior, vp_ref[:, lanes], 1, 0) + dot_on(own, v_ref[:, lanes], 1, 0)
+        ).astype(o_ref.dtype)
+
+
+def attention_call(queries, prior_keys, prior_values, keys_in, values_in):
+    rows, width = queries.shape
+    heads = width // AD
+    group = 2 * AD if heads % 2 == 0 else AD
+    spec = pl.BlockSpec((rows, group), lambda h: (0, h))
+    return pl.pallas_call(
+        attention_body,
+        grid=(width // group,),
+        in_specs=[spec] * 5,
+        out_specs=spec,
+        out_shape=jax.ShapeDtypeStruct(queries.shape, jnp.float32),
+        compiler_params=pltpu.CompilerParams(vmem_limit_bytes=VMEM_LIMIT),
+        name="attention",
+    )(queries, prior_keys, prior_values, keys_in, values_in)
+
+
+def newton_step(y_ref, kind):
+    first, second, third = NEWTON_COEFFS
+    matrix = y_ref[kind]
+    gram = dot_on(matrix, matrix, 1, 1).astype(jnp.bfloat16)
+    square = dot_on(gram, gram, 1, 0)
+    poly = (second * gram.astype(jnp.float32) + third * square).astype(jnp.bfloat16)
+    y_ref[kind] = (first * matrix.astype(jnp.float32) + dot_on(poly, matrix, 1, 0)).astype(
+        jnp.bfloat16
+    )
+
+
+def update_body(span, seq_count, g_ref, wg_ref, wu_ref, wd_ref, *refs):
+    last = span == SPANS - 1
+    outs = refs[: 1 if last else KINDS]
+    (near, total, far, x_ref, y_ref, new_ref) = refs[len(outs) : len(outs) + 6]
+    (send_near, recv_near, send_far, recv_far, pair_sem, send_out, recv_out, ready) = refs[
+        len(outs) + 6 :
+    ]
+    w_refs = (wg_ref, wu_ref, wd_ref)
+    per_span = seq_count // SPANS
+    chips = per_span // 2
+    feature = g_ref.shape[-1]
+    half = feature // 2
+    me = lax.axis_index("seq")
+    my_span = me // per_span
+    place = me % per_span
+    chip = place // 2
+    core = place % 2
+    mate = me + 1 - 2 * core
+    column = chip % 2
+    layer = chip // 2
+    own_rows = pl.ds(pl.multiple_of(core * half, half), half)
+    mate_rows = pl.ds(pl.multiple_of((1 - core) * half, half), half)
+    in_span = my_span == span
+
+    def remote(src, dst, send, recv, device):
+        return pltpu.make_async_remote_copy(
+            src_ref=src, dst_ref=dst, send_sem=send, recv_sem=recv,
+            device_id={"seq": device}, device_id_type=MESH,
+        )
+
+    def at_place(which_span, which_chip):
+        return which_span * per_span + 2 * which_chip + core
+
+    barrier = pltpu.get_barrier_semaphore()
+    if last:
+        for step in range(1, seq_count):
+            pl.semaphore_signal(
+                barrier, inc=1, device_id={"seq": (me + step) % seq_count}, device_id_type=MESH
+            )
+        pl.semaphore_wait(barrier, seq_count - 1)
+    else:
+        for step in range(1, per_span):
+            peer = my_span * per_span + (place + step) % per_span
+            pl.semaphore_signal(barrier, inc=1, device_id={"seq": peer}, device_id_type=MESH)
+
+        @pl.when(in_span)
+        def _():
+            pl.semaphore_signal(
+                barrier, inc=1, device_id={"seq": at_place(span + 1, column)}, device_id_type=MESH
+            )
+
+        @pl.when(in_span)
+        def _():
+            pl.semaphore_wait(barrier, per_span - 1)
+
+        @pl.when(jnp.logical_not(in_span) & (layer == 0))
+        def _():
+            pl.semaphore_wait(barrier, per_span - 1 + 2)
+
+        @pl.when(jnp.logical_not(in_span) & (layer != 0))
+        def _():
+            pl.semaphore_wait(barrier, per_span - 1)
+
+    @pl.when(in_span)
+    def _():
+        targets = [(chip + step) % chips for step in range(1, chips)] + [chip]
+        near_copies = []
+        for slot, target in enumerate(targets):
+            copy = remote(
+                g_ref.at[:, target, mate_rows], near.at[:, slot],
+                send_near.at[slot], recv_near.at[slot], mate,
+            )
+            copy.start()
+            near_copies.append(copy)
+        far_copies = []
+        for slot, target in enumerate(targets[:-1]):
+            near_copies[slot].wait_recv()
+            for kind in range(KINDS):
+                total[kind, slot] = (
+                    g_ref[kind, target, own_rows].astype(jnp.float32)
+                    + near[kind, slot].astype(jnp.float32)
+                ).astype(jnp.bfloat16)
+            copy = remote(
+                total.at[:, slot], far.at[:, slot], send_far.at[slot], recv_far.at[slot],
+                at_place(span, target),
+            )
+            copy.start()
+            far_copies.append(copy)
+        if not last:
+            for kind in range(KINDS):
+                outs[kind][...] = w_refs[kind][...]
+        near_copies[-1].wait_recv()
+        for copy in far_copies:
+            copy.wait_recv()
+        for kind in range(KINDS):
+            summed = g_ref[kind, chip, own_rows].astype(jnp.float32)
+            summed = summed + near[kind, chips - 1].astype(jnp.float32)
+            for slot in range(chips - 1):
+                summed = summed + far[kind, slot].astype(jnp.float32)
+            x_ref[kind, own_rows] = summed.astype(jnp.bfloat16)
+        pair = remote(
+            x_ref.at[:, own_rows], x_ref.at[:, own_rows], pair_sem.at[0], pair_sem.at[1], mate
+        )
+        pair.start()
+        for copy in near_copies:
+            copy.wait_send()
+        for copy in far_copies:
+            copy.wait_send()
+        pair.wait()
+        if not last:
+            pl.semaphore_wait(ready, 1)
+        out_copies = []
+        for kind in range(KINDS):
+            gathered = x_ref[kind].astype(jnp.float32)
+            norm = jnp.sqrt(jnp.sum(gathered * gathered, keepdims=True) + 1e-06)
+            y_ref[kind] = (gathered / norm).astype(jnp.bfloat16)
+
+            @pl.loop(0, NS_STEPS)
+            def _(step):
+                newton_step(y_ref, kind)
+
+            unmoved = w_refs[kind][chip].astype(jnp.float32)
+            moved = unmoved - y_ref[kind].astype(jnp.float32)
+            target = jnp.sqrt(jnp.sum(unmoved * unmoved, axis=0, keepdims=True) + 1e-06)
+            current = jnp.sqrt(jnp.sum(moved * moved, axis=0, keepdims=True) + 1e-06)
+            new_ref[kind] = (moved * (target / current)).astype(jnp.bfloat16)
+            if not last:
+                copy = remote(
+                    new_ref.at[kind, own_rows], outs[kind].at[chip, own_rows],
+                    send_out.at[0, kind, 0], recv_out.at[core, kind, chip],
+                    at_place(span + 1, column),
+                )
+                copy.start()
+                out_copies.append(copy)
+        if last:
+            share = feature // seq_count
+            chip_count = seq_count // 2
+            here = pl.ds(pl.multiple_of(me * share, share), share)
+            for step in range(1, chip_count):
+                device = 2 * ((me // 2 + step) % chip_count) + core
+                there = pl.ds(pl.multiple_of(device * share, share), share)
+                copy = remote(
+                    new_ref.at[:, there], outs[0].at[:, chip],
+                    send_out.at[step], recv_out.at[chip], device,
+                )
+                copy.start()
+                out_copies.append(copy)
+            for kind in range(KINDS):
+                outs[0][kind, chip] = new_ref[kind, here]
+        for copy in out_copies:
+            copy.wait_send()
+
+    if last:
+        for owner in range(chips):
+            @pl.when(jnp.logical_not(in_span & (chip == owner)))
+            def _():
+                remote(
+                    new_ref.at[:, pl.ds(0, feature // seq_count)], outs[0].at[:, owner],
+                    send_out.at[0], recv_out.at[owner], mate,
+                ).wait_recv()
+        return
+
+    @pl.when(jnp.logical_not(in_span))
+    def _():
+        @pl.when(layer == 0)
+        def _():
+            for owner_layer in range(2):
+                pl.semaphore_signal(
+                    ready, inc=1, device_id={"seq": at_place(span, 2 * owner_layer + column)},
+                    device_id_type=MESH,
+                )
+
+        def passing(kind, owner, lane, device):
+            block = outs[kind].at[owner, own_rows]
+            return remote(
+                block, block, send_out.at[lane, kind, owner], recv_out.at[core, kind, owner], device
+            )
+
+        chunks = [(kind, owner_layer) for kind in range(KINDS) for owner_layer in (1, 0)]
+        across = at_place(my_span, 2 * layer + 1 - column)
+        beyond = at_place(my_span, 2 + column)
+
+        def cross_chunk(kind, owner_layer):
+            to_mate = passing(kind, 2 * owner_layer + 1 - column, 0, mate)
+            to_mate.wait_recv()
+            to_mate.start()
+
+        for number, (kind, owner_layer) in enumerate(chunks):
+            owner = 2 * owner_layer + column
+            passing(kind, owner, 0, mate).wait_recv()
+
+            @pl.when(layer == 0)
+            def _():
+                passing(kind, owner, 2, beyond).start()
+
+            passing(kind, owner, 1, across).start()
+            passing(kind, owner, 0, mate).start()
+            if number:
+                cross_chunk(*chunks[number - 1])
+        cross_chunk(*chunks[-1])
+        for kind, owner_layer in chunks:
+            for owner in (2 * owner_layer + column, 2 * owner_layer + 1 - column):
+                other = outs[kind].at[owner, mate_rows]
+                remote(
+                    other, other, send_out.at[0, kind, owner],
+                    recv_out.at[1 - core, kind, owner], mate,
+                ).wait_recv()
+                passing(kind, owner, 0, mate).wait_send()
+            owner = 2 * owner_layer + column
+            passing(kind, owner, 1, across).wait_send()
+
+            @pl.when(layer == 0)
+            def _():
+                passing(kind, owner, 2, beyond).wait_send()
+
+
+def update_call(span, seq_count, grads, weights):
+    last = span == SPANS - 1
+    _, heads, feature, _ = grads.shape
+    chips = seq_count // SPANS // 2
+    half = feature // 2
+    vmem = pl.BlockSpec(memory_space=pltpu.VMEM)
+    if last:
+        out_shape = [
+            jax.ShapeDtypeStruct((KINDS, heads, feature // seq_count, feature), jnp.bfloat16)
+        ]
+        out_sems = [
+            pltpu.SemaphoreType.DMA((seq_count // 2,)),
+            pltpu.SemaphoreType.DMA((chips,)),
+        ]
+    else:
+        out_shape = [jax.ShapeDtypeStruct(weights[0].shape, jnp.bfloat16)] * KINDS
+        out_sems = [
+            pltpu.SemaphoreType.DMA((3, KINDS, heads)),
+            pltpu.SemaphoreType.DMA((2, KINDS, heads)),
+        ]
+    return pl.pallas_call(
+        functools.partial(update_body, span, seq_count),
+        out_shape=out_shape,
+        in_specs=[vmem] * 4,
+        out_specs=[vmem] * len(out_shape),
+        scratch_shapes=[
+            pltpu.VMEM((KINDS, chips, half, feature), jnp.bfloat16),
+            pltpu.VMEM((KINDS, chips - 1, half, feature), jnp.bfloat16),
+            pltpu.VMEM((KINDS, chips - 1, half, feature), jnp.bfloat16),
+            pltpu.VMEM((KINDS, feature, feature), jnp.bfloat16),
+            pltpu.VMEM((KINDS, feature, feature), jnp.bfloat16),
+            pltpu.VMEM((KINDS, feature, feature), jnp.bfloat16),
+            pltpu.SemaphoreType.DMA((chips,)),
+            pltpu.SemaphoreType.DMA((chips,)),
+            pltpu.SemaphoreType.DMA((chips - 1,)),
+            pltpu.SemaphoreType.DMA((chips - 1,)),
+            pltpu.SemaphoreType.DMA((2,)),
+            *out_sems,
+            pltpu.SemaphoreType.REGULAR,
+        ],
+        compiler_params=pltpu.CompilerParams(
+            collective_id=span, has_side_effects=True, vmem_limit_bytes=VMEM_LIMIT
+        ),
+        cost_estimate=pl.CostEstimate(
+            flops=60_000_000_000, bytes_accessed=2**28, transcendentals=0
+        ),
+        name=f"update{span}",
+    )(grads, *weights)
+
+
+def owned_on_device(
+    fast_q, fast_k, fast_v, rates, w_gate, w_up, w_down, w_out, att_q, att_k, att_v
+):
+    seq_count = lax.axis_size("seq")
+    early = lax.axis_index("seq") < seq_count // SPANS
+    start = (w_gate, w_up, w_down)
+    rate_cols = rates[:, :, None]
+    heads, feature, _ = w_gate.shape
+    prior_k = passed_along(att_k, "seq", 1)
+    prior_v = passed_along(att_v, "seq", 1)
+
+    def attention():
+        return attention_call(att_q, prior_k, prior_v, att_k, att_v)
+
+    def slopes(weights):
+        return gradient_call(weights, fast_k, fast_v, rate_cols)
+
+    grads = lax.cond(
+        early,
+        lambda: slopes(start),
+        lambda: jnp.zeros((KINDS, heads, feature, feature), jnp.bfloat16),
+    )
+    waited = lax.cond(early, lambda: jnp.zeros(att_q.shape, jnp.float32), attention)
+    grads, waited = lax.optimization_barrier((grads, waited))
+    weights = update_call(0, seq_count, grads, start)
+    grads, attended = lax.cond(
+        early,
+        lambda: (grads, attention()),
+        lambda: (slopes(weights), waited),
+    )
+    fast_rows = apply_call(weights, fast_q)
+    partial_out = jnp.dot(fast_rows, w_out, preferred_element_type=jnp.float32)
+    partial_out = partial_out.astype(jnp.bfloat16)
+    grads, partial_out = lax.optimization_barrier((grads, partial_out))
+    fast_sum = lax.psum_scatter(partial_out, "head", scatter_dimension=1, tiled=True)
+    (final_weights,) = update_call(1, seq_count, grads, weights)
+    return ((attended + fast_sum.astype(jnp.float32)).astype(jnp.bfloat16), final_weights)
+
+
 def solution(mesh):
     in_specs = (
         P("seq", "head"),
@@ -153,6 +584,12 @@
         P("seq", "head"),
     )
     out_specs = (P("seq", "head"), P(None, "head", "seq", None))
+    owned = mesh.shape["seq"] == 4 * 2 * SPANS
+
+    def either(*arrays):
+        held = arrays[4].shape[0] == mesh.shape["seq"] // (2 * SPANS)
+        return (owned_on_device if owned and held else on_device)(*arrays)
+
     return jax.shard_map(
-        on_device, mesh=mesh, in_specs=in_specs, out_specs=out_specs, check_vma=False
+        either, mesh=mesh, in_specs=in_specs, out_specs=out_specs, check_vma=False
     )

time: 504 us -> 279 us (0.55); the launches traced: 496 us -> 278 us
  Pallas kernels: 0 us -> 222 us
  waiting for transfers between devices: 209 us -> 17.1 us
  matrix products: 175 us -> 13.8 us
  other arithmetic: 62.8 us -> 2.67 us
  local copies, waits for them, and re-layouts: 28.6 us -> 1.96 us
    pallas_call x0 -> x5, Pallas kernels: none -> 222 us  [the longest x2 195 us: update_call(): pl.pallas_call(functools.partial(update_body, span, seq_count), out_shape...]
    psum x2 -> x0, waiting for transfers between devices: 209 us -> none  [on_device(): summed = lax.psum(stacked.astype(jnp.bfloat16), 'seq').astype(jnp.float32)]
    dot_general x25 -> x1, matrix products: 175 us -> 13.8 us  [owned_on_device(): partial_out = jnp.dot(fast_rows, w_out, preferred_element_type=jnp.float32)]
    reduce_sum x4 -> x0, other arithmetic: 20.9 us -> none  [the longest x2 12.5 us: renorm(): current = jnp.sqrt(jnp.sum(moved * moved, axis=1, keepdims=True) + 1e-06)]
    unnamed x47 -> x11, local copies, waits for them, and re-layouts: 21.3 us -> 0.77 us
    convert_element_type x7 -> x1, other arithmetic: 22.5 us -> 2.67 us  [owned_on_device(): (attended + fast_sum.astype(jnp.float32)).astype(jnp.bfloat16)]
    ppermute x2, waiting for transfers between devices: 0.01 us -> 17.1 us  [passed_along(): return lax.ppermute(block, axis, route)]
    sub x1 -> x0, other arithmetic: 15.4 us -> none  [attend(): exp_scores = jnp.exp(scores - row_max)]
  transfers between devices with their start and end apart: 5 -> 3, of which waited for: 2 -> 2; matrix products, arithmetic and copies ran while one was open for 34% -> 0% of each run, Pallas kernels for 0% -> 41%
where the time goes in v1:
time: 279 us; the launch traced here: 278 us
  Pallas kernels  222 us (80%)
  waiting for transfers between devices  17.1 us (6%)
  between operations  14.2 us (5%)
  matrix products  13.8 us (5%)
  starting transfers between devices  5.67 us (2%)
    pallas_call x2, Pallas kernels, update_call(): pl.pallas_call(functools.partial(update_body, span, seq_count), out_shape...  195 us
    ppermute x2, waiting for transfers between devices, passed_along(): return lax.ppermute(block, axis, route)  17.1 us
    dot_general x1, matrix products, owned_on_device(): partial_out = jnp.dot(fast_rows, w_out, preferred_element_type=jnp.float32)  13.8 us
    pallas_call x1, Pallas kernels, attention_call(): pl.pallas_call(attention_body, grid=(width // group,), in_specs=[spec] *...  12.4 us
    pallas_call x1, Pallas kernels, gradient_call(): pl.pallas_call(gradient_body, grid=(heads,), in_specs=[rows_spec, rows_sp...  8.94 us
    ppermute x2, starting transfers between devices, passed_along(): return lax.ppermute(block, axis, route)  5.64 us
  transfers between devices with their start and end apart: 3, of which 2 were waited for; matrix products, arithmetic and copies ran while one was open for 0% of the time, Pallas kernels for 41%

profile of v1, /device:TPU:11, one launch (start us, length us, event | category | flops | bytes accessed | tf_op | source)
XLA Modules:
  0.0 277.7 jit_solution(2378082177417046912)
XLA Ops:
  7.2 0.0 reduce-scatter.2.cloned.1.call-start
  7.2 3.7 %collective-permute-start = (bf16[256,2560]{1,0:T(8,128)(2,1)}, bf16[256,2560]{1,0:T(8,128)(2,1)}, u32[]{:S(2)}, u32[]{:S(2)}) collective-permute-start(bf16[256,2560]{1,0:T(8,128)(2,1)} %param.26), channel_id=1, source_target_pairs={{0,2},{2,4},{4,6},{6,8},{8,10},{10,12},{12,14},{14,16},{16,18},{18... | collective-permute-start | bytes 3932168 | tf_op jit(solution)/shard_map/ppermute | solution.py:24
  10.9 1.9 collective-permute-start.1
  12.9 9.9 %conditional.3 = (bf16[3,4,512,512]{3,2,1,0:T(8,128)(2,1)}) conditional(s32[]{:T(128)} %convert_element_type.14, () %tuple.30, (bf16[256,2048]{1,0:T(8,128)(2,1)}, bf16[256,2048]{1,0:T(8,128)(2,1)}, f32[4,256,1]{1,0,2:T(4,128)}, bf16[4,512,512]{2,1,0:T(8,128)(2,1)}, bf16[4,512,512]{2,1,0:T(8,128)(2,1)}, ...), branch_computations={%region_0.0_spmd, %region_1.0_spmd} | conditional | bytes 6291466 | solution.py:550
  12.9 0.9 copy.13.r_ref
  13.8 8.9 %gradients.2 = bf16[3,4,512,512]{3,2,1,0:T(8,128)(2,1)} custom-call(bf16[256,2048]{1,0:T(8,128)(2,1)} %get-tuple-element.48.k_ref, bf16[256,2048]{1,0:T(8,128)(2,1)} %get-tuple-element.49.v_ref, f32[4,256,1]{2,1,0:T(8,128)S(1)} %copy.13.r_ref, bf16[4,512,512]{2,1,0:T(8,128)(2,1)} %get-tuple-element.57.wg_ref, bf16[4,512,512]{2,1,0:T(8,128)(2,1)} %get-tuple-element.58.wu_ref, ...), custom_call_target="tpu_custom_call" | custom-call | tf_op jit(solution)/shard_map/cond/branch_1_fun/gradients/pallas_call | solution.py:176
  22.7 3.0 %collective-permute-done = bf16[256,2560]{1,0:T(8,128)(2,1)} collective-permute-done((bf16[256,2560]{1,0:T(8,128)(2,1)}, bf16[256,2560]{1,0:T(8,128)(2,1)}, u32[]{:S(2)}, u32[]{:S(2)}) %collective-permute-start) | collective-permute-done | bytes 1310752 | tf_op jit(solution)/shard_map/ppermute | solution.py:24
  25.8 14.0 %collective-permute-done.1 = bf16[256,2560]{1,0:T(8,128)(2,1)} collective-permute-done((bf16[256,2560]{1,0:T(8,128)(2,1)}, bf16[256,2560]{1,0:T(8,128)(2,1)}, u32[]{:S(2)}, u32[]{:S(2)}) %collective-permute-start.1) | collective-permute-done | bytes 1310752 | tf_op jit(solution)/shard_map/ppermute | solution.py:24
  39.8 0.3 conditional.4
  39.8 0.3 broadcast.5
  40.1 0.0 copy-start
  40.1 90.6 %update0.1 = (bf16[4,512,512]{2,1,0:T(8,128)(2,1)}, bf16[4,512,512]{2,1,0:T(8,128)(2,1)}, bf16[4,512,512]{2,1,0:T(8,128)(2,1)}) custom-call(bf16[3,4,512,512]{3,2,1,0:T(8,128)(2,1)} %get-tuple-element.119.g_ref, bf16[4,512,512]{2,1,0:T(8,128)(2,1)} %wg_ref.1, bf16[4,512,512]{2,1,0:T(8,128)(2,1)} %wu_ref.1, bf16[4,512,512]{2,1,0:T(8,128)(2,1)} %wd_ref.1), custom_call_target="tpu_custom_call" | custom-call | flops 60000002048 | bytes 268435456 | tf_op jit(solution)/shard_map/update0/pallas_call | solution.py:503
  130.7 0.0 copy-start.2
  130.7 0.0 copy-start.3
  130.8 0.0 copy-start.4
  130.8 5.5 %fast_apply.1 = bf16[256,2048]{1,0:T(8,128)(2,1)S(1)} custom-call(bf16[256,2048]{1,0:T(8,128)(2,1)} %q_ref.1, bf16[4,512,512]{2,1,0:T(8,128)(2,1)} %get-tuple-element.90.wg_ref, bf16[4,512,512]{2,1,0:T(8,128)(2,1)} %get-tuple-element.91.wu_ref, bf16[4,512,512]{2,1,0:T(8,128)(2,1)} %get-tuple-element.92.wd_ref), custom_call_target="tpu_custom_call" | custom-call | tf_op jit(solution)/shard_map/fast_apply/pallas_call | solution.py:203
  136.3 12.4 %conditional.5 = (bf16[3,4,512,512]{3,2,1,0:T(8,128)(2,1)}, f32[256,2560]{1,0:T(8,128)}) conditional(s32[]{:T(128)} %convert_element_type.14, (bf16[256,2048]{1,0:T(8,128)(2,1)}, bf16[256,2048]{1,0:T(8,128)(2,1)}, f32[4,256,1]{1,0,2:T(4,128)S(1)}, bf16[4,512,512]{2,1,0:T(8,128)(2,1)}, bf16[4,512,512]{2,1,0:T(8,128)(2,1)}, ...), branch_computations={%region_4.0_spmd, %region_5.0_spmd} | conditional | bytes 8208 | solution.py:558
  136.3 12.4 %attention.3 = f32[256,2560]{1,0:T(8,128)} custom-call(bf16[256,2560]{1,0:T(8,128)(2,1)S(1)} %get-tuple-element.73.q_ref, bf16[256,2560]{1,0:T(8,128)(2,1)} %get-tuple-element.74.kp_ref, bf16[256,2560]{1,0:T(8,128)(2,1)} %get-tuple-element.75.vp_ref, bf16[256,2560]{1,0:T(8,128)(2,1)S(1)} %get-tuple-element.76.k_ref, bf16[256,2560]{1,0:T(8,128)(2,1)} %get-tuple-element.77.v_ref), custom_call_target="tpu_custom_call" | custom-call | tf_op jit(solution)/shard_map/cond/branch_1_fun/attention/pallas_call | solution.py:245
  148.8 13.8 %convolution_convert_fusion = bf16[256,5120]{1,0:T(8,128)(2,1)} fusion(bf16[256,2048]{1,0:T(8,128)(2,1)S(1)} %fast_apply.1, bf16[2048,5120]{1,0:T(8,128)(2,1)} %param.24), kind=kOutput, calls=%fused_computation | convolution fusion | flops 5370019840 | bytes 24641536 | tf_op jit(solution)/shard_map/dot_general | solution.py:564
  162.6 0.0 reduce-scatter.2.cloned.1.call-update
  162.6 104.7 %update1.1 = bf16[3,4,32,512]{3,2,1,0:T(8,128)(2,1)S(1)} custom-call(bf16[3,4,512,512]{3,2,1,0:T(8,128)(2,1)} %get-tuple-element.97.g_ref, bf16[4,512,512]{2,1,0:T(8,128)(2,1)} %get-tuple-element.90.wg_ref, bf16[4,512,512]{2,1,0:T(8,128)(2,1)} %get-tuple-element.91.wu_ref, bf16[4,512,512]{2,1,0:T(8,128)(2,1)} %get-tuple-element.92.wd_ref), custom_call_target="tpu_custom_call" | custom-call | flops 60000002048 | bytes 268435456 | tf_op jit(solution)/shard_map/update1/pallas_call | solution.py:503
  267.4 0.0 reduce-scatter.2.cloned.1.call-done
  267.4 2.7 add_convert_fusion
  270.1 0.7 copy.24
  (6 shorter events, 0.0 us)
Async XLA Ops:
  7.2 260.2 %reduce-scatter.2.cloned.1.call-start = ((), (), s32[]{:S(2)}) async-start(), calls=%async_computation.1 | async-start | bytes 3932160 | tf_op jit(solution)/shard_map/reduce_scatter | solution.py:567
  7.2 18.6 %collective-permute-start = (bf16[256,2560]{1,0:T(8,128)(2,1)}, bf16[256,2560]{1,0:T(8,128)(2,1)}, u32[]{:S(2)}, u32[]{:S(2)}) collective-permute-start(bf16[256,2560]{1,0:T(8,128)(2,1)} %param.26), channel_id=1, source_target_pairs={{0,2},{2,4},{4,6},{6,8},{8,10},{10,12},{12,14},{14,16},{16,18},{18... | collective-permute-start | bytes 3932168 | tf_op jit(solution)/shard_map/ppermute | solution.py:24
  10.9 28.9 %collective-permute-start.1 = (bf16[256,2560]{1,0:T(8,128)(2,1)}, bf16[256,2560]{1,0:T(8,128)(2,1)}, u32[]{:S(2)}, u32[]{:S(2)}) collective-permute-start(bf16[256,2560]{1,0:T(8,128)(2,1)} %param.27), channel_id=1, source_target_pairs={{0,2},{2,4},{4,6},{6,8},{8,10},{10,12},{12,14},{14,16},{16,18},{18... | collective-permute-start | bytes 3932168 | tf_op jit(solution)/shard_map/ppermute | solution.py:24
  40.1 90.6 %copy-start = (f32[256,2560]{1,0:T(8,128)}, f32[256,2560]{1,0:T(8,128)S(1)}, u32[]{:S(2)}) copy-start(f32[256,2560]{1,0:T(8,128)S(1)} %get-tuple-element.120) | copy-start | bytes 7864324
  130.7 5.6 %copy-start.2 = (bf16[256,2560]{1,0:T(8,128)(2,1)S(1)}, bf16[256,2560]{1,0:T(8,128)(2,1)}, u32[]{:S(2)}) copy-start(bf16[256,2560]{1,0:T(8,128)(2,1)} %param.25) | copy-start | bytes 3932164
  130.7 5.6 %copy-start.3 = (bf16[256,2560]{1,0:T(8,128)(2,1)S(1)}, bf16[256,2560]{1,0:T(8,128)(2,1)}, u32[]{:S(2)}) copy-start(bf16[256,2560]{1,0:T(8,128)(2,1)} %param.26) | copy-start | bytes 3932164
  130.8 5.6 %copy-start.4 = (f32[4,256]{1,0:T(4,128)S(1)}, f32[4,256]{1,0:T(4,128)}, u32[]{:S(2)}) copy-start(f32[4,256]{1,0:T(4,128)} %param.20) | copy-start | bytes 12292
  162.6 104.8 %copy-start.1 = (f32[256,2560]{1,0:T(8,128)S(1)}, f32[256,2560]{1,0:T(8,128)}, u32[]{:S(2)}) copy-start(f32[256,2560]{1,0:T(8,128)} %get-tuple-element.94) | copy-start | bytes 7864324
Sparse Core Ops, SparseCore 0:
  162.7 66.8 reduce-scatter.1

commit v2 on v1

--- a/solution.py
+++ b/solution.py
@@ -330,53 +330,50 @@
     @pl.when(in_span)
     def _():
         targets = [(chip + step) % chips for step in range(1, chips)] + [chip]
-        near_copies = []
-        for slot, target in enumerate(targets):
-            copy = remote(
-                g_ref.at[:, target, mate_rows], near.at[:, slot],
-                send_near.at[slot], recv_near.at[slot], mate,
+
+        def near_copy(kind, slot):
+            return remote(
+                g_ref.at[kind, targets[slot], mate_rows], near.at[kind, slot],
+                send_near.at[kind, slot], recv_near.at[kind, slot], mate,
             )
-            copy.start()
-            near_copies.append(copy)
-        far_copies = []
-        for slot, target in enumerate(targets[:-1]):
-            near_copies[slot].wait_recv()
-            for kind in range(KINDS):
+
+        def far_copy(kind, slot):
+            return remote(
+                total.at[kind, slot], far.at[kind, slot],
+                send_far.at[kind, slot], recv_far.at[kind, slot], at_place(span, targets[slot]),
+            )
+
+        def pair_copy(kind):
+            return remote(
+                x_ref.at[kind, own_rows], x_ref.at[kind, own_rows],
+                pair_sem.at[0, kind], pair_sem.at[1, kind], mate,
+            )
+
+        for kind in range(KINDS):
+            for slot in range(chips):
+                near_copy(kind, slot).start()
+        for kind in range(KINDS):
+            for slot, target in enumerate(targets[:-1]):
+                near_copy(kind, slot).wait_recv()
                 total[kind, slot] = (
                     g_ref[kind, target, own_rows].astype(jnp.float32)
                     + near[kind, slot].astype(jnp.float32)
                 ).astype(jnp.bfloat16)
-            copy = remote(
-                total.at[:, slot], far.at[:, slot], send_far.at[slot], recv_far.at[slot],
-                at_place(span, target),
-            )
-            copy.start()
-            far_copies.append(copy)
+                far_copy(kind, slot).start()
+            near_copy(kind, chips - 1).wait_recv()
         if not last:
             for kind in range(KINDS):
                 outs[kind][...] = w_refs[kind][...]
-        near_copies[-1].wait_recv()
-        for copy in far_copies:
-            copy.wait_recv()
+        out_copies = []
         for kind in range(KINDS):
             summed = g_ref[kind, chip, own_rows].astype(jnp.float32)
             summed = summed + near[kind, chips - 1].astype(jnp.float32)
             for slot in range(chips - 1):
+                far_copy(kind, slot).wait_recv()
                 summed = summed + far[kind, slot].astype(jnp.float32)
             x_ref[kind, own_rows] = summed.astype(jnp.bfloat16)
-        pair = remote(
-            x_ref.at[:, own_rows], x_ref.at[:, own_rows], pair_sem.at[0], pair_sem.at[1], mate
-        )
-        pair.start()
-        for copy in near_copies:
-            copy.wait_send()
-        for copy in far_copies:
-            copy.wait_send()
-        pair.wait()
-        if not last:
-            pl.semaphore_wait(ready, 1)
-        out_copies = []
-        for kind in range(KINDS):
+            pair_copy(kind).start()
+            pair_copy(kind).wait()
             gathered = x_ref[kind].astype(jnp.float32)
             norm = jnp.sqrt(jnp.sum(gathered * gathered, keepdims=True) + 1e-06)
             y_ref[kind] = (gathered / norm).astype(jnp.bfloat16)
@@ -391,6 +388,8 @@
             current = jnp.sqrt(jnp.sum(moved * moved, axis=0, keepdims=True) + 1e-06)
             new_ref[kind] = (moved * (target / current)).astype(jnp.bfloat16)
             if not last:
+                if kind == 0:
+                    pl.semaphore_wait(ready, 1)
                 copy = remote(
                     new_ref.at[kind, own_rows], outs[kind].at[chip, own_rows],
                     send_out.at[0, kind, 0], recv_out.at[core, kind, chip],
@@ -398,32 +397,38 @@
                 )
                 copy.start()
                 out_copies.append(copy)
-        if last:
+                continue
             share = feature // seq_count
             chip_count = seq_count // 2
-            here = pl.ds(pl.multiple_of(me * share, share), share)
             for step in range(1, chip_count):
                 device = 2 * ((me // 2 + step) % chip_count) + core
                 there = pl.ds(pl.multiple_of(device * share, share), share)
                 copy = remote(
-                    new_ref.at[:, there], outs[0].at[:, chip],
-                    send_out.at[step], recv_out.at[chip], device,
+                    new_ref.at[kind, there], outs[0].at[kind, chip],
+                    send_out.at[kind, step], recv_out.at[kind, chip], device,
                 )
                 copy.start()
                 out_copies.append(copy)
-            for kind in range(KINDS):
-                outs[0][kind, chip] = new_ref[kind, here]
+            here = pl.ds(pl.multiple_of(me * share, share), share)
+            outs[0][kind, chip] = new_ref[kind, here]
         for copy in out_copies:
             copy.wait_send()
+        for kind in range(KINDS):
+            for slot in range(chips):
+                near_copy(kind, slot).wait_send()
+            for slot in range(chips - 1):
+                far_copy(kind, slot).wait_send()
 
     if last:
         for owner in range(chips):
             @pl.when(jnp.logical_not(in_span & (chip == owner)))
             def _():
-                remote(
-                    new_ref.at[:, pl.ds(0, feature // seq_count)], outs[0].at[:, owner],
-                    send_out.at[0], recv_out.at[owner], mate,
-                ).wait_recv()
+                for kind in range(KINDS):
+                    remote(
+                        new_ref.at[kind, pl.ds(0, feature // seq_count)],
+                        outs[0].at[kind, owner],
+                        send_out.at[kind, 0], recv_out.at[kind, owner], mate,
+                    ).wait_recv()
         return
 
     @pl.when(jnp.logical_not(in_span))
@@ -491,8 +496,8 @@
             jax.ShapeDtypeStruct((KINDS, heads, feature // seq_count, feature), jnp.bfloat16)
         ]
         out_sems = [
-            pltpu.SemaphoreType.DMA((seq_count // 2,)),
-            pltpu.SemaphoreType.DMA((chips,)),
+            pltpu.SemaphoreType.DMA((KINDS, seq_count // 2)),
+            pltpu.SemaphoreType.DMA((KINDS, chips)),
         ]
     else:
         out_shape = [jax.ShapeDtypeStruct(weights[0].shape, jnp.bfloat16)] * KINDS
@@ -512,11 +517,11 @@
             pltpu.VMEM((KINDS, feature, feature), jnp.bfloat16),
             pltpu.VMEM((KINDS, feature, feature), jnp.bfloat16),
             pltpu.VMEM((KINDS, feature, feature), jnp.bfloat16),
-            pltpu.SemaphoreType.DMA((chips,)),
-            pltpu.SemaphoreType.DMA((chips,)),
-            pltpu.SemaphoreType.DMA((chips - 1,)),
-            pltpu.SemaphoreType.DMA((chips - 1,)),
-            pltpu.SemaphoreType.DMA((2,)),
+            pltpu.SemaphoreType.DMA((KINDS, chips)),
+            pltpu.SemaphoreType.DMA((KINDS, chips)),
+            pltpu.SemaphoreType.DMA((KINDS, chips - 1)),
+            pltpu.SemaphoreType.DMA((KINDS, chips - 1)),
+            pltpu.SemaphoreType.DMA((2, KINDS)),
             *out_sems,
             pltpu.SemaphoreType.REGULAR,
         ],
@@ -538,11 +543,14 @@
     start = (w_gate, w_up, w_down)
     rate_cols = rates[:, :, None]
     heads, feature, _ = w_gate.shape
-    prior_k = passed_along(att_k, "seq", 1)
-    prior_v = passed_along(att_v, "seq", 1)
-
-    def attention():
-        return attention_call(att_q, prior_k, prior_v, att_k, att_v)
+    count = seq_count // SPANS
+
+    def prior_of(blocks, low, high):
+        route = [(i - 1, i) for i in range(max(low, 1), high)]
+        return tuple(lax.ppermute(block, "seq", route) for block in blocks)
+
+    def attention(prior):
+        return attention_call(att_q, *prior, att_k, att_v)
 
     def slopes(weights):
         return gradient_call(weights, fast_k, fast_v, rate_cols)
@@ -552,12 +560,17 @@
         lambda: slopes(start),
         lambda: jnp.zeros((KINDS, heads, feature, feature), jnp.bfloat16),
     )
-    waited = lax.cond(early, lambda: jnp.zeros(att_q.shape, jnp.float32), attention)
+    prior = prior_of((att_k, att_v), count, seq_count)
+    waited = lax.cond(
+        early, lambda: jnp.zeros(att_q.shape, jnp.float32), lambda: attention(prior)
+    )
     grads, waited = lax.optimization_barrier((grads, waited))
     weights = update_call(0, seq_count, grads, start)
+    weights, later = lax.optimization_barrier((weights, (att_k, att_v)))
+    early_prior = prior_of(later, 0, count)
     grads, attended = lax.cond(
         early,
-        lambda: (grads, attention()),
+        lambda: (grads, attention(early_prior)),
         lambda: (slopes(weights), waited),
     )
     fast_rows = apply_call(weights, fast_q)

time: 279 us -> 234 us (0.84)
  Pallas kernels: 222 us -> 184 us
  waiting for transfers between devices: 17.1 us -> 8.61 us
  starting transfers between devices: 5.67 us -> 8.71 us
    pallas_call x2, Pallas kernels: 195 us -> 158 us  [update_call(): pl.pallas_call(functools.partial(update_body, span, seq_count), out_shape...]
    ppermute x2 -> x4, waiting for transfers between devices: 17.1 us -> 8.58 us  [prior_of(): return tuple((lax.ppermute(block, 'seq', route) for block in blocks))]
    ppermute x2 -> x4, starting transfers between devices: 5.64 us -> 8.68 us  [prior_of(): return tuple((lax.ppermute(block, 'seq', route) for block in blocks))]
  transfers between devices with their start and end apart: 3 -> 5, of which waited for: 2 -> 1; matrix products, arithmetic and copies ran while one was open for 0% -> 6% of each run, Pallas kernels for 41% -> 36%
where the time goes in v2:
time: 234 us
  Pallas kernels  184 us (79%)
  between operations  14.2 us (6%)
  matrix products  13.9 us (6%)
  starting transfers between devices  8.71 us (4%)
  waiting for transfers between devices  8.61 us (4%)
  other arithmetic  2.67 us (1%)
    pallas_call x2, Pallas kernels, update_call(): pl.pallas_call(functools.partial(update_body, span, seq_count), out_shape...  158 us
    dot_general x1, matrix products, owned_on_device(): partial_out = jnp.dot(fast_rows, w_out, preferred_element_type=jnp.float32)  13.9 us
    pallas_call x1, Pallas kernels, attention_call(): pl.pallas_call(attention_body, grid=(width // group,), in_specs=[spec] *...  11.9 us
    pallas_call x1, Pallas kernels, gradient_call(): pl.pallas_call(gradient_body, grid=(heads,), in_specs=[rows_spec, rows_sp...  8.96 us
    ppermute x4, starting transfers between devices, prior_of(): return tuple((lax.ppermute(block, 'seq', route) for block in blocks))  8.68 us
    ppermute x4, waiting for transfers between devices, prior_of(): return tuple((lax.ppermute(block, 'seq', route) for block in blocks))  8.58 us
  transfers between devices with their start and end apart: 5, of which 1 were waited for; matrix products, arithmetic and copies ran while one was open for 6% of the time, Pallas kernels for 36%

profile of v2, /device:TPU:11, one launch (start us, length us, event | category | flops | bytes accessed | tf_op | source)
XLA Modules:
  0.0 233.6 jit_solution(8775298417899104430)
XLA Ops:
  7.2 0.0 reduce-scatter.2.cloned.1.call-start
  7.2 0.7 collective-permute-start
  8.0 1.7 collective-permute-start.1
  9.7 9.9 %conditional.3 = (bf16[3,4,512,512]{3,2,1,0:T(8,128)(2,1)}) conditional(s32[]{:T(128)} %convert_element_type.14, () %tuple.31, (bf16[256,2048]{1,0:T(8,128)(2,1)}, bf16[256,2048]{1,0:T(8,128)(2,1)}, f32[4,256,1]{1,0,2:T(4,128)}, bf16[4,512,512]{2,1,0:T(8,128)(2,1)}, bf16[4,512,512]{2,1,0:T(8,128)(2,1)}, ...), branch_computations={%region_0.0_spmd, %region_1.0_spmd} | conditional | bytes 6291466 | solution.py:558
  9.7 0.9 copy.13.r_ref
  10.6 9.0 %gradients.2 = bf16[3,4,512,512]{3,2,1,0:T(8,128)(2,1)} custom-call(bf16[256,2048]{1,0:T(8,128)(2,1)} %get-tuple-element.48.k_ref, bf16[256,2048]{1,0:T(8,128)(2,1)} %get-tuple-element.49.v_ref, f32[4,256,1]{2,1,0:T(8,128)S(1)} %copy.13.r_ref, bf16[4,512,512]{2,1,0:T(8,128)(2,1)} %get-tuple-element.57.wg_ref, bf16[4,512,512]{2,1,0:T(8,128)(2,1)} %get-tuple-element.58.wu_ref, ...), custom_call_target="tpu_custom_call" | custom-call | tf_op jit(solution)/shard_map/cond/branch_1_fun/gradients/pallas_call | solution.py:176
  19.6 0.0 collective-permute-done
  19.6 0.0 collective-permute-done.1
  19.6 0.3 conditional.4
  19.6 0.3 broadcast.5
  19.9 86.6 %update0.1 = (bf16[4,512,512]{2,1,0:T(8,128)(2,1)S(1)}, bf16[4,512,512]{2,1,0:T(8,128)(2,1)S(1)}, bf16[4,512,512]{2,1,0:T(8,128)(2,1)S(1)}) custom-call(bf16[3,4,512,512]{3,2,1,0:T(8,128)(2,1)} %get-tuple-element.129.g_ref, bf16[4,512,512]{2,1,0:T(8,128)(2,1)} %wg_ref.1, bf16[4,512,512]{2,1,0:T(8,128)(2,1)} %wu_ref.1, bf16[4,512,512]{2,1,0:T(8,128)(2,1)} %wd_ref.1), custom_call_target="tpu_custom_call" | custom-call | flops 60000002048 | bytes 268435456 | tf_op jit(solution)/shard_map/update0/pallas_call | solution.py:508
  106.5 4.1 %collective-permute-start.2 = (bf16[256,2560]{1,0:T(8,128)(2,1)}, bf16[256,2560]{1,0:T(8,128)(2,1)}, u32[]{:S(2)}, u32[]{:S(2)}) collective-permute-start(bf16[256,2560]{1,0:T(8,128)(2,1)} %param.26), channel_id=1, source_target_pairs={{0,2},{2,4},{4,6},{6,8},{8,10},{10,12},{12,14},{1,3},{3,5},{5,7},{... | collective-permute-start | bytes 3932168 | tf_op jit(solution)/shard_map/ppermute | solution.py:550
  110.6 2.1 collective-permute-start.3
  112.7 4.2 %fast_apply.1 = bf16[256,2048]{1,0:T(8,128)(2,1)S(1)} custom-call(bf16[256,2048]{1,0:T(8,128)(2,1)} %q_ref.1, bf16[4,512,512]{2,1,0:T(8,128)(2,1)S(1)} %get-tuple-element.98.wg_ref, bf16[4,512,512]{2,1,0:T(8,128)(2,1)S(1)} %get-tuple-element.99.wu_ref, bf16[4,512,512]{2,1,0:T(8,128)(2,1)S(1)} %get-tuple-element.100.wd_ref), custom_call_target="tpu_custom_call" | custom-call | tf_op jit(solution)/shard_map/fast_apply/pallas_call | solution.py:203
  117.0 0.0 copy-start.4
  117.0 13.9 %convolution_convert_fusion = bf16[256,5120]{1,0:T(8,128)(2,1)} fusion(bf16[256,2048]{1,0:T(8,128)(2,1)S(1)} %fast_apply.1, bf16[2048,5120]{1,0:T(8,128)(2,1)} %param.24), kind=kOutput, calls=%fused_computation | convolution fusion | flops 5370019840 | bytes 24641536 | tf_op jit(solution)/shard_map/dot_general | solution.py:577
  131.0 8.6 %collective-permute-done.3 = bf16[256,2560]{1,0:T(8,128)(2,1)} collective-permute-done((bf16[256,2560]{1,0:T(8,128)(2,1)}, bf16[256,2560]{1,0:T(8,128)(2,1)}, u32[]{:S(2)}, u32[]{:S(2)}) %collective-permute-start.3) | collective-permute-done | bytes 1310752 | tf_op jit(solution)/shard_map/ppermute | solution.py:550
  139.5 11.9 %conditional.5 = (bf16[3,4,512,512]{3,2,1,0:T(8,128)(2,1)}, f32[256,2560]{1,0:T(8,128)S(1)}) conditional(s32[]{:T(128)} %convert_element_type.14, (bf16[256,2048]{1,0:T(8,128)(2,1)}, bf16[256,2048]{1,0:T(8,128)(2,1)}, f32[4,256,1]{1,0,2:T(4,128)S(1)}, bf16[4,512,512]{2,1,0:T(8,128)(2,1)}, bf16[4,512,512]{2,1,0:T(8,128)(2,1)}, ...), branch_computations={%region_4.0_spmd, %region_5.0_spmd} | conditional | bytes 8208 | solution.py:571
  139.5 11.9 %attention.3 = f32[256,2560]{1,0:T(8,128)S(1)} custom-call(bf16[256,2560]{1,0:T(8,128)(2,1)} %get-tuple-element.73.q_ref, bf16[256,2560]{1,0:T(8,128)(2,1)} %get-tuple-element.74.kp_ref, bf16[256,2560]{1,0:T(8,128)(2,1)} %get-tuple-element.75.vp_ref, bf16[256,2560]{1,0:T(8,128)(2,1)} %get-tuple-element.76.k_ref, bf16[256,2560]{1,0:T(8,128)(2,1)} %get-tuple-element.77.v_ref), custom_call_target="tpu_custom_call" | custom-call | tf_op jit(solution)/shard_map/cond/branch_1_fun/attention/pallas_call | solution.py:245
  151.4 0.0 reduce-scatter.2.cloned.1.call-update
  151.5 71.8 %update1.1 = bf16[3,4,32,512]{3,2,1,0:T(8,128)(2,1)S(1)} custom-call(bf16[3,4,512,512]{3,2,1,0:T(8,128)(2,1)} %get-tuple-element.107.g_ref, bf16[4,512,512]{2,1,0:T(8,128)(2,1)} %copy-done, bf16[4,512,512]{2,1,0:T(8,128)(2,1)} %copy-done.1, bf16[4,512,512]{2,1,0:T(8,128)(2,1)} %copy-done.2), custom_call_target="tpu_custom_call" | custom-call | flops 60000002048 | bytes 268435456 | tf_op jit(solution)/shard_map/update1/pallas_call | solution.py:508
  223.3 0.0 reduce-scatter.2.cloned.1.call-done
  223.3 2.7 %add_convert_fusion = bf16[256,2560]{1,0:T(8,128)(2,1)} fusion(f32[256,2560]{1,0:T(8,128)S(1)} %get-tuple-element.104, bf16[256,2560]{1,0:T(8,128)(2,1)} %reduce-scatter.2.cloned.1.call-done), kind=kLoop, calls=%fused_computation.1 | loop fusion | flops 1966080 | bytes 5242880 | tf_op jit(solution)/shard_map/convert_element_type | solution.py:582
  226.0 0.7 copy.24
  (8 shorter events, 0.0 us)
Async XLA Ops:
  7.2 216.1 %reduce-scatter.2.cloned.1.call-start = ((), (), s32[]{:S(2)}) async-start(), calls=%async_computation.1 | async-start | bytes 3932160 | tf_op jit(solution)/shard_map/reduce_scatter | solution.py:580
  7.2 12.4 %collective-permute-start = (bf16[256,2560]{1,0:T(8,128)(2,1)}, bf16[256,2560]{1,0:T(8,128)(2,1)S(1)}, u32[]{:S(2)}, u32[]{:S(2)}) collective-permute-start(bf16[256,2560]{1,0:T(8,128)(2,1)} %param.26), channel_id=1, source_target_pairs={{14,16},{16,18},{18,20},{20,22},{22,24},{24,26},{26,28},{28,30},{1... | collective-permute-start | bytes 3932168 | tf_op jit(solution)/shard_map/ppermute | solution.py:550
  8.0 11.6 %collective-permute-start.1 = (bf16[256,2560]{1,0:T(8,128)(2,1)}, bf16[256,2560]{1,0:T(8,128)(2,1)}, u32[]{:S(2)}, u32[]{:S(2)}) collective-permute-start(bf16[256,2560]{1,0:T(8,128)(2,1)} %param.27), channel_id=1, source_target_pairs={{14,16},{16,18},{18,20},{20,22},{22,24},{24,26},{26,28},{28,30},{1... | collective-permute-start | bytes 3932168 | tf_op jit(solution)/shard_map/ppermute | solution.py:550
  106.5 10.5 %copy-start = (bf16[4,512,512]{2,1,0:T(8,128)(2,1)}, bf16[4,512,512]{2,1,0:T(8,128)(2,1)S(1)}, u32[]{:S(2)}) copy-start(bf16[4,512,512]{2,1,0:T(8,128)(2,1)S(1)} %get-tuple-element.98.wg_ref) | copy-start | bytes 6291460
  106.5 10.5 %copy-start.1 = (bf16[4,512,512]{2,1,0:T(8,128)(2,1)}, bf16[4,512,512]{2,1,0:T(8,128)(2,1)S(1)}, u32[]{:S(2)}) copy-start(bf16[4,512,512]{2,1,0:T(8,128)(2,1)S(1)} %get-tuple-element.99.wu_ref) | copy-start | bytes 6291460
  106.5 10.5 %copy-start.2 = (bf16[4,512,512]{2,1,0:T(8,128)(2,1)}, bf16[4,512,512]{2,1,0:T(8,128)(2,1)S(1)}, u32[]{:S(2)}) copy-start(bf16[4,512,512]{2,1,0:T(8,128)(2,1)S(1)} %get-tuple-element.100.wd_ref) | copy-start | bytes 6291460
  106.5 24.4 %collective-permute-start.2 = (bf16[256,2560]{1,0:T(8,128)(2,1)}, bf16[256,2560]{1,0:T(8,128)(2,1)}, u32[]{:S(2)}, u32[]{:S(2)}) collective-permute-start(bf16[256,2560]{1,0:T(8,128)(2,1)} %param.26), channel_id=1, source_target_pairs={{0,2},{2,4},{4,6},{6,8},{8,10},{10,12},{12,14},{1,3},{3,5},{5,7},{... | collective-permute-start | bytes 3932168 | tf_op jit(solution)/shard_map/ppermute | solution.py:550
  110.6 28.9 %collective-permute-start.3 = (bf16[256,2560]{1,0:T(8,128)(2,1)}, bf16[256,2560]{1,0:T(8,128)(2,1)}, u32[]{:S(2)}, u32[]{:S(2)}) collective-permute-start(bf16[256,2560]{1,0:T(8,128)(2,1)} %param.27), channel_id=1, source_target_pairs={{0,2},{2,4},{4,6},{6,8},{8,10},{10,12},{12,14},{1,3},{3,5},{5,7},{... | collective-permute-start | bytes 3932168 | tf_op jit(solution)/shard_map/ppermute | solution.py:550
  117.0 22.5 %copy-start.4 = (f32[4,256]{1,0:T(4,128)S(1)}, f32[4,256]{1,0:T(4,128)}, u32[]{:S(2)}) copy-start(f32[4,256]{1,0:T(4,128)} %param.20) | copy-start | bytes 12292
Sparse Core Ops, SparseCore 0:
  151.6 50.7 reduce-scatter.1

commit v3 on v2

--- a/solution.py
+++ b/solution.py
@@ -209,6 +209,28 @@
         compiler_params=pltpu.CompilerParams(vmem_limit_bytes=VMEM_LIMIT),
         name="fast_apply",
     )(queries, *weights)
+
+
+def projection_body(rows_ref, w_ref, o_ref):
+    o_ref[...] = dot_on(rows_ref[...], w_ref[...], 1, 0).astype(o_ref.dtype)
+
+
+def projection_call(fast_rows, w_out):
+    rows, depth = fast_rows.shape
+    width = w_out.shape[1]
+    tile = next(size for size in (512, 256, 128, width) if width % size == 0)
+    return pl.pallas_call(
+        projection_body,
+        grid=(width // tile,),
+        in_specs=[
+            pl.BlockSpec((rows, depth), lambda j: (0, 0)),
+            pl.BlockSpec((depth, tile), lambda j: (0, j)),
+        ],
+        out_specs=pl.BlockSpec((rows, tile), lambda j: (0, j)),
+        out_shape=jax.ShapeDtypeStruct((rows, width), jnp.bfloat16),
+        compiler_params=pltpu.CompilerParams(vmem_limit_bytes=VMEM_LIMIT),
+        name="projection",
+    )(fast_rows, w_out)
 
 
 def attention_body(q_ref, kp_ref, vp_ref, k_ref, v_ref, o_ref):
@@ -574,8 +596,7 @@
         lambda: (slopes(weights), waited),
     )
     fast_rows = apply_call(weights, fast_q)
-    partial_out = jnp.dot(fast_rows, w_out, preferred_element_type=jnp.float32)
-    partial_out = partial_out.astype(jnp.bfloat16)
+    partial_out = projection_call(fast_rows, w_out)
     grads, partial_out = lax.optimization_barrier((grads, partial_out))
     fast_sum = lax.psum_scatter(partial_out, "head", scatter_dimension=1, tiled=True)
     (final_weights,) = update_call(1, seq_count, grads, weights)

time: 234 us -> 235 us (level)
  Pallas kernels: 184 us -> 198 us
  matrix products: 13.9 us -> 0 us
    pallas_call x0 -> x1, Pallas kernels: none -> 14 us  [projection_call(): pl.pallas_call(projection_body, grid=(width // tile,), in_specs=[pl.Block...]
    dot_general x1 -> x0, matrix products: 13.9 us -> none  [owned_on_device(): partial_out = jnp.dot(fast_rows, w_out, preferred_element_type=jnp.float32)]
  transfers between devices with their start and end apart: 5 -> 5, of which waited for: 1 -> 1; matrix products, arithmetic and copies ran while one was open for 6% -> 0% of each run, Pallas kernels for 36% -> 42%
where the time goes in v3:
time: 235 us; the launch traced here: 234 us
  Pallas kernels  198 us (84%)
  between operations  14.2 us (6%)
  waiting for transfers between devices  8.71 us (4%)
  starting transfers between devices  8.53 us (4%)
  other arithmetic  2.67 us (1%)
    pallas_call x2, Pallas kernels, update_call(): pl.pallas_call(functools.partial(update_body, span, seq_count), out_shape...  159 us
    pallas_call x1, Pallas kernels, projection_call(): pl.pallas_call(projection_body, grid=(width // tile,), in_specs=[pl.Block...  14 us
    pallas_call x1, Pallas kernels, attention_call(): pl.pallas_call(attention_body, grid=(width // group,), in_specs=[spec] *...  11.9 us
    pallas_call x1, Pallas kernels, gradient_call(): pl.pallas_call(gradient_body, grid=(heads,), in_specs=[rows_spec, rows_sp...  8.96 us
    ppermute x4, waiting for transfers between devices, prior_of(): return tuple((lax.ppermute(block, 'seq', route) for block in blocks))  8.67 us
    ppermute x4, starting transfers between devices, prior_of(): return tuple((lax.ppermute(block, 'seq', route) for block in blocks))  8.5 us
  transfers between devices with their start and end apart: 5, of which 1 were waited for; matrix products, arithmetic and copies ran while one was open for 0% of the time, Pallas kernels for 42%

profile of v3, /device:TPU:11, one launch (start us, length us, event | category | flops | bytes accessed | tf_op | source)
XLA Modules:
  0.0 233.8 jit_solution(11011984326685135267)
XLA Ops:
  7.2 0.0 reduce-scatter.2.cloned.1.call-start
  7.2 0.7 collective-permute-start
  8.0 1.7 collective-permute-start.1
  9.7 9.9 %conditional.3 = (bf16[3,4,512,512]{3,2,1,0:T(8,128)(2,1)}) conditional(s32[]{:T(128)} %convert_element_type.11, () %tuple.31, (bf16[256,2048]{1,0:T(8,128)(2,1)}, bf16[256,2048]{1,0:T(8,128)(2,1)}, f32[4,256,1]{1,0,2:T(4,128)}, bf16[4,512,512]{2,1,0:T(8,128)(2,1)}, bf16[4,512,512]{2,1,0:T(8,128)(2,1)}, ...), branch_computations={%region_0.0_spmd, %region_1.0_spmd} | conditional | bytes 6291466 | solution.py:580
  9.7 0.9 copy.13.r_ref
  10.6 9.0 %gradients.2 = bf16[3,4,512,512]{3,2,1,0:T(8,128)(2,1)} custom-call(bf16[256,2048]{1,0:T(8,128)(2,1)} %get-tuple-element.48.k_ref, bf16[256,2048]{1,0:T(8,128)(2,1)} %get-tuple-element.49.v_ref, f32[4,256,1]{2,1,0:T(8,128)S(1)} %copy.13.r_ref, bf16[4,512,512]{2,1,0:T(8,128)(2,1)} %get-tuple-element.57.wg_ref, bf16[4,512,512]{2,1,0:T(8,128)(2,1)} %get-tuple-element.58.wu_ref, ...), custom_call_target="tpu_custom_call" | custom-call | tf_op jit(solution)/shard_map/cond/branch_1_fun/gradients/pallas_call | solution.py:176
  19.6 0.0 collective-permute-done
  19.6 0.0 collective-permute-done.1
  19.6 0.3 conditional.4
  19.6 0.3 broadcast.5
  19.9 86.6 %update0.1 = (bf16[4,512,512]{2,1,0:T(8,128)(2,1)S(1)}, bf16[4,512,512]{2,1,0:T(8,128)(2,1)S(1)}, bf16[4,512,512]{2,1,0:T(8,128)(2,1)S(1)}) custom-call(bf16[3,4,512,512]{3,2,1,0:T(8,128)(2,1)} %get-tuple-element.129.g_ref, bf16[4,512,512]{2,1,0:T(8,128)(2,1)} %wg_ref.1, bf16[4,512,512]{2,1,0:T(8,128)(2,1)} %wu_ref.1, bf16[4,512,512]{2,1,0:T(8,128)(2,1)} %wd_ref.1), custom_call_target="tpu_custom_call" | custom-call | flops 60000002048 | bytes 268435456 | tf_op jit(solution)/shard_map/update0/pallas_call | solution.py:530
  106.5 4.1 %collective-permute-start.2 = (bf16[256,2560]{1,0:T(8,128)(2,1)}, bf16[256,2560]{1,0:T(8,128)(2,1)}, u32[]{:S(2)}, u32[]{:S(2)}) collective-permute-start(bf16[256,2560]{1,0:T(8,128)(2,1)} %param.26), channel_id=1, source_target_pairs={{0,2},{2,4},{4,6},{6,8},{8,10},{10,12},{12,14},{1,3},{3,5},{5,7},{... | collective-permute-start | bytes 3932168 | tf_op jit(solution)/shard_map/ppermute | solution.py:572
  110.6 1.9 collective-permute-start.3
  112.6 4.2 %fast_apply.1.rows_ref = bf16[256,2048]{1,0:T(8,128)(2,1)S(1)} custom-call(bf16[256,2048]{1,0:T(8,128)(2,1)} %q_ref.1, bf16[4,512,512]{2,1,0:T(8,128)(2,1)S(1)} %get-tuple-element.98.wg_ref, bf16[4,512,512]{2,1,0:T(8,128)(2,1)S(1)} %get-tuple-element.99.wu_ref, bf16[4,512,512]{2,1,0:T(8,128)(2,1)S(1)} %get-tuple-element.100.wd_ref), custom_call_target="tpu_custom_call" | custom-call | tf_op jit(solution)/shard_map/fast_apply/pallas_call | solution.py:203
  116.8 0.0 copy-start.4
  116.8 14.0 %projection.1 = bf16[256,5120]{1,0:T(8,128)(2,1)} custom-call(bf16[256,2048]{1,0:T(8,128)(2,1)S(1)} %fast_apply.1.rows_ref, bf16[2048,5120]{1,0:T(8,128)(2,1)} %w_ref.1), custom_call_target="tpu_custom_call" | custom-call | tf_op jit(solution)/shard_map/projection/pallas_call | solution.py:222
  130.9 8.7 %collective-permute-done.3 = bf16[256,2560]{1,0:T(8,128)(2,1)} collective-permute-done((bf16[256,2560]{1,0:T(8,128)(2,1)}, bf16[256,2560]{1,0:T(8,128)(2,1)}, u32[]{:S(2)}, u32[]{:S(2)}) %collective-permute-start.3) | collective-permute-done | bytes 1310752 | tf_op jit(solution)/shard_map/ppermute | solution.py:572
  139.5 11.9 %conditional.5 = (bf16[3,4,512,512]{3,2,1,0:T(8,128)(2,1)}, f32[256,2560]{1,0:T(8,128)S(1)}) conditional(s32[]{:T(128)} %convert_element_type.11, (bf16[256,2048]{1,0:T(8,128)(2,1)}, bf16[256,2048]{1,0:T(8,128)(2,1)}, f32[4,256,1]{1,0,2:T(4,128)S(1)}, bf16[4,512,512]{2,1,0:T(8,128)(2,1)}, bf16[4,512,512]{2,1,0:T(8,128)(2,1)}, ...), branch_computations={%region_4.0_spmd, %region_5.0_spmd} | conditional | bytes 8208 | solution.py:593
  139.5 11.9 %attention.3 = f32[256,2560]{1,0:T(8,128)S(1)} custom-call(bf16[256,2560]{1,0:T(8,128)(2,1)} %get-tuple-element.73.q_ref, bf16[256,2560]{1,0:T(8,128)(2,1)} %get-tuple-element.74.kp_ref, bf16[256,2560]{1,0:T(8,128)(2,1)} %get-tuple-element.75.vp_ref, bf16[256,2560]{1,0:T(8,128)(2,1)} %get-tuple-element.76.k_ref, bf16[256,2560]{1,0:T(8,128)(2,1)} %get-tuple-element.77.v_ref), custom_call_target="tpu_custom_call" | custom-call | tf_op jit(solution)/shard_map/cond/branch_1_fun/attention/pallas_call | solution.py:267
  151.4 0.0 reduce-scatter.2.cloned.1.call-update
  151.5 72.1 %update1.1 = bf16[3,4,32,512]{3,2,1,0:T(8,128)(2,1)S(1)} custom-call(bf16[3,4,512,512]{3,2,1,0:T(8,128)(2,1)} %get-tuple-element.107.g_ref, bf16[4,512,512]{2,1,0:T(8,128)(2,1)} %copy-done, bf16[4,512,512]{2,1,0:T(8,128)(2,1)} %copy-done.1, bf16[4,512,512]{2,1,0:T(8,128)(2,1)} %copy-done.2), custom_call_target="tpu_custom_call" | custom-call | flops 60000002048 | bytes 268435456 | tf_op jit(solution)/shard_map/update1/pallas_call | solution.py:530
  223.5 0.0 reduce-scatter.2.cloned.1.call-done
  223.6 2.7 %add_convert_fusion = bf16[256,2560]{1,0:T(8,128)(2,1)} fusion(f32[256,2560]{1,0:T(8,128)S(1)} %get-tuple-element.104, bf16[256,2560]{1,0:T(8,128)(2,1)} %reduce-scatter.2.cloned.1.call-done), kind=kLoop, calls=%fused_computation | loop fusion | flops 1966080 | bytes 5242880 | tf_op jit(solution)/shard_map/convert_element_type | solution.py:603
  226.2 0.7 copy.24
  (8 shorter events, 0.0 us)
Async XLA Ops:
  7.2 216.4 %reduce-scatter.2.cloned.1.call-start = ((), (), s32[]{:S(2)}) async-start(), calls=%async_computation.1 | async-start | bytes 3932160 | tf_op jit(solution)/shard_map/reduce_scatter | solution.py:601
  7.2 12.4 %collective-permute-start = (bf16[256,2560]{1,0:T(8,128)(2,1)}, bf16[256,2560]{1,0:T(8,128)(2,1)S(1)}, u32[]{:S(2)}, u32[]{:S(2)}) collective-permute-start(bf16[256,2560]{1,0:T(8,128)(2,1)} %param.26), channel_id=1, source_target_pairs={{14,16},{16,18},{18,20},{20,22},{22,24},{24,26},{26,28},{28,30},{1... | collective-permute-start | bytes 3932168 | tf_op jit(solution)/shard_map/ppermute | solution.py:572
  8.0 11.6 %collective-permute-start.1 = (bf16[256,2560]{1,0:T(8,128)(2,1)}, bf16[256,2560]{1,0:T(8,128)(2,1)}, u32[]{:S(2)}, u32[]{:S(2)}) collective-permute-start(bf16[256,2560]{1,0:T(8,128)(2,1)} %param.27), channel_id=1, source_target_pairs={{14,16},{16,18},{18,20},{20,22},{22,24},{24,26},{26,28},{28,30},{1... | collective-permute-start | bytes 3932168 | tf_op jit(solution)/shard_map/ppermute | solution.py:572
  106.5 10.3 %copy-start = (bf16[4,512,512]{2,1,0:T(8,128)(2,1)}, bf16[4,512,512]{2,1,0:T(8,128)(2,1)S(1)}, u32[]{:S(2)}) copy-start(bf16[4,512,512]{2,1,0:T(8,128)(2,1)S(1)} %get-tuple-element.98.wg_ref) | copy-start | bytes 6291460
  106.5 10.3 %copy-start.1 = (bf16[4,512,512]{2,1,0:T(8,128)(2,1)}, bf16[4,512,512]{2,1,0:T(8,128)(2,1)S(1)}, u32[]{:S(2)}) copy-start(bf16[4,512,512]{2,1,0:T(8,128)(2,1)S(1)} %get-tuple-element.99.wu_ref) | copy-start | bytes 6291460
  106.5 10.3 %copy-start.2 = (bf16[4,512,512]{2,1,0:T(8,128)(2,1)}, bf16[4,512,512]{2,1,0:T(8,128)(2,1)S(1)}, u32[]{:S(2)}) copy-start(bf16[4,512,512]{2,1,0:T(8,128)(2,1)S(1)} %get-tuple-element.100.wd_ref) | copy-start | bytes 6291460
  106.5 24.3 %collective-permute-start.2 = (bf16[256,2560]{1,0:T(8,128)(2,1)}, bf16[256,2560]{1,0:T(8,128)(2,1)}, u32[]{:S(2)}, u32[]{:S(2)}) collective-permute-start(bf16[256,2560]{1,0:T(8,128)(2,1)} %param.26), channel_id=1, source_target_pairs={{0,2},{2,4},{4,6},{6,8},{8,10},{10,12},{12,14},{1,3},{3,5},{5,7},{... | collective-permute-start | bytes 3932168 | tf_op jit(solution)/shard_map/ppermute | solution.py:572
  110.6 28.9 %collective-permute-start.3 = (bf16[256,2560]{1,0:T(8,128)(2,1)}, bf16[256,2560]{1,0:T(8,128)(2,1)}, u32[]{:S(2)}, u32[]{:S(2)}) collective-permute-start(bf16[256,2560]{1,0:T(8,128)(2,1)} %param.27), channel_id=1, source_target_pairs={{0,2},{2,4},{4,6},{6,8},{8,10},{10,12},{12,14},{1,3},{3,5},{5,7},{... | collective-permute-start | bytes 3932168 | tf_op jit(solution)/shard_map/ppermute | solution.py:572
  116.8 22.7 %copy-start.4 = (f32[4,256]{1,0:T(4,128)S(1)}, f32[4,256]{1,0:T(4,128)}, u32[]{:S(2)}) copy-start(f32[4,256]{1,0:T(4,128)} %param.20) | copy-start | bytes 12292
Sparse Core Ops, SparseCore 0:
  151.6 51.0 reduce-scatter.1
